TPU v7x, 512 devices: a whole 4x4x16 slice. The times are simulated.
512 devices in a mesh: gx: 32 (over y_hi, z), gy: 4 (over x), gz: 4 (over y_lo, core).
Axes of the slice: x: 4, y: 4 (y_hi: 2, y_lo: 2; y = y_hi * 2 + y_lo), z: 16, core: 2. Of those that a mesh axis runs over, the one named last changes fastest.
Arguments:
- fields: float32 [12, 256, 32, 512], P(None, 'gx', 'gy', 'gz'), as said below
- reacting: int32 [256, 32, 512], P('gx', 'gy', 'gz'), may hold values from 0 to 1, as said below
- panel_map: int32 [2, 256, 512], P(None, 'gx', 'gz'), may hold values from 0 to 4095, as said below
- layer_one: bfloat16 [1600, 12], replicated, may hold values from -4 to 4
- layer_two: bfloat16 [800, 1600], replicated, may hold values from -0.21875 to 0.21875
- layer_three: bfloat16 [400, 800], replicated, may hold values from -0.3125 to 0.3125
- layer_four: bfloat16 [12, 400], replicated, may hold values from -0.3125 to 0.3125
Outputs:
- new_fields: float32 [12, 256, 32, 512], P(None, 'gx', 'gy', 'gz')
- impulse: float32 [4096], P(('gx', 'gy', 'gz'))
Inputs may be any that keep to these rules, and one draw needn't show every extreme that they name: `fields`: component 0 (density) lies between 0.3 and 3.3; the velocities (components 1 to 3 over component 0) between -1.2 and 1.2; the pressure 0.4 (component 4 - |momentum|^2 / (2 density)) between 0.3 and 5; components 5 to 11 are 0.01 to 0.14 times component 0. Each device's aligned block of 8 x 8 x 128 cells holds at most 256 reacting cells. The blocks that share their ranges along the second and third dimensions hold exactly 64 reacting cells each on average, and one in eight of them, and at least one, hold exactly 256. `panel_map`: every panel is a patch of 8 x 8 cells of one wall, shifted by 4 cells along the first dimension and closed around it; panels are numbered in a random order and each number is used once.
All inputs are finite; a program needn't handle non-finite values.
Results may differ from a plain program's by a relative error of at most 0.0014.
Values may be sent and summed in bfloat16 or wider, within the bound.
A program may use at most 64 MiB of HBM per device.

v0:
```python
import jax
import jax.numpy as jnp
from jax import lax
from jax.sharding import PartitionSpec as P

BAL = 64
COMPS = 12
PATCH = 8


HEAT_RATIO = 1.4
TIME_STEP = 0.1
CHEM_STEP = 0.25
WENO_EPS = 1e-06


def extended(array, sides, width):
    for axis, dim in sides:
        size, length = (lax.axis_size(axis), array.shape[dim])
        up = [(i, (i + 1) % size) for i in range(size - 1)]
        down = [(j, i) for i, j in up]
        last = lax.slice_in_dim(array, length - width, length, axis=dim)
        initial = lax.slice_in_dim(array, 0, width, axis=dim)
        before = lax.ppermute(last, axis, up)
        after = lax.ppermute(initial, axis, down)
        array = jnp.concatenate([before, array, after], axis=dim)
    return array


def take_slab(array_in, begin_at, length_of, flux_axis):
    return lax.slice_in_dim(array_in, begin_at, begin_at + length_of, axis=flux_axis)


def weno_face(upwind_two, upwind_one, center, downwind_one, downwind_two):
    cand_zero = (2.0 * upwind_two - 7.0 * upwind_one + 11.0 * center) / 6.0
    cand_one = (-upwind_one + 5.0 * center + 2.0 * downwind_one) / 6.0
    cand_two = (2.0 * center + 5.0 * downwind_one - downwind_two) / 6.0
    smooth_zero = (
        13.0 / 12.0 * (upwind_two - 2.0 * upwind_one + center) ** 2
        + 0.25 * (upwind_two - 4.0 * upwind_one + 3.0 * center) ** 2
    )
    smooth_one = (
        13.0 / 12.0 * (upwind_one - 2.0 * center + downwind_one) ** 2
        + 0.25 * (upwind_one - downwind_one) ** 2
    )
    smooth_two = (
        13.0 / 12.0 * (center - 2.0 * downwind_one + downwind_two) ** 2
        + 0.25 * (3.0 * center - 4.0 * downwind_one + downwind_two) ** 2
    )
    weight_zero = 0.1 / (WENO_EPS + smooth_zero) ** 2
    weight_one = 0.6 / (WENO_EPS + smooth_one) ** 2
    weight_two = 0.3 / (WENO_EPS + smooth_two) ** 2
    weight_sum = weight_zero + weight_one + weight_two
    return (weight_zero * cand_zero + weight_one * cand_one + weight_two * cand_two) / weight_sum


def to_recon(fields):
    density = fields[0]
    velocity = fields[1:4] / density[None]
    pressure = (HEAT_RATIO - 1.0) * (
        fields[4] - 0.5 * density * jnp.sum(velocity * velocity, axis=0)
    )
    fractions = fields[5:] / density[None]
    return jnp.concatenate(
        [jnp.log(density)[None], velocity, jnp.log(pressure)[None], fractions], axis=0
    )


def normal_of(normal, ndims):
    return (jnp.arange(3) == normal).reshape((3,) + (1,) * (ndims - 1))


def side_terms(recon, normal):
    density = jnp.exp(recon[0])
    velocity = recon[1:4]
    pressure = jnp.exp(recon[4])
    fractions = recon[5:]
    speed_n = velocity[normal]
    energy = pressure / (HEAT_RATIO - 1.0) + 0.5 * density * jnp.sum(velocity * velocity, axis=0)
    conserved = jnp.concatenate(
        [density[None], density[None] * velocity, energy[None], density[None] * fractions], axis=0
    )
    mass_flux = density * speed_n
    normal_mask = normal_of(normal, recon.ndim)
    momentum_flux = mass_flux[None] * velocity + jnp.where(normal_mask, pressure[None], 0.0)
    flux_terms = jnp.concatenate(
        [
            mass_flux[None],
            momentum_flux,
            ((energy + pressure) * speed_n)[None],
            mass_flux[None] * fractions,
        ],
        axis=0,
    )
    sound_speed = jnp.sqrt(HEAT_RATIO * pressure / density)
    return (
        density,
        velocity,
        pressure,
        fractions,
        energy,
        conserved,
        flux_terms,
        speed_n,
        sound_speed,
    )


def star_state(
    density, velocity, pressure, fractions, energy, speed_n, wave_speed, contact, normal_mask
):
    relative = wave_speed - speed_n
    factor = density * relative / (wave_speed - contact)
    star_velocity = jnp.where(normal_mask, contact[None], velocity)
    star_energy = energy / density + (contact - speed_n) * (
        contact + pressure / (density * relative)
    )
    return jnp.concatenate(
        [
            factor[None],
            factor[None] * star_velocity,
            (factor * star_energy)[None],
            factor[None] * fractions,
        ],
        axis=0,
    )


def hllc_flux(left_recon, right_recon, normal):
    (
        left_density,
        left_velocity,
        left_pressure,
        left_fractions,
        left_energy,
        left_cons,
        left_flux,
        left_speed,
        left_sound,
    ) = side_terms(left_recon, normal)
    (
        right_density,
        right_velocity,
        right_pressure,
        right_fractions,
        right_energy,
        right_cons,
        right_flux,
        right_speed,
        right_sound,
    ) = side_terms(right_recon, normal)
    wave_left = jnp.minimum(left_speed - left_sound, right_speed - right_sound)
    wave_right = jnp.maximum(left_speed + left_sound, right_speed + right_sound)
    left_rel = wave_left - left_speed
    right_rel = wave_right - right_speed
    contact = (
        right_pressure
        - left_pressure
        + left_density * left_speed * left_rel
        - right_density * right_speed * right_rel
    ) / (left_density * left_rel - right_density * right_rel)
    normal_mask = normal_of(normal, left_recon.ndim)
    star_left = star_state(
        left_density,
        left_velocity,
        left_pressure,
        left_fractions,
        left_energy,
        left_speed,
        wave_left,
        contact,
        normal_mask,
    )
    star_right = star_state(
        right_density,
        right_velocity,
        right_pressure,
        right_fractions,
        right_energy,
        right_speed,
        wave_right,
        contact,
        normal_mask,
    )
    left_star_flux = left_flux + wave_left[None] * (star_left - left_cons)
    right_star_flux = right_flux + wave_right[None] * (star_right - right_cons)
    return jnp.where(
        wave_left[None] >= 0,
        left_flux,
        jnp.where(
            contact[None] >= 0,
            left_star_flux,
            jnp.where(wave_right[None] > 0, right_star_flux, right_flux),
        ),
    )


def face_flux(padded, normal):
    flux_axis = normal + 1
    face_count = padded.shape[flux_axis] - 5
    stencil = [take_slab(padded, offset, face_count, flux_axis) for offset in range(6)]
    left_state = weno_face(stencil[0], stencil[1], stencil[2], stencil[3], stencil[4])
    right_state = weno_face(stencil[5], stencil[4], stencil[3], stencil[2], stencil[1])
    return hllc_flux(left_state, right_state, normal)


def mirror_walls(padded, normal, at_first, at_last):
    flux_axis = normal + 1
    cell_count = padded.shape[flux_axis] - 6
    flip_sign = (
        jnp.where(jnp.arange(padded.shape[0]) == 1 + normal, -1.0, 1.0)
        .astype(padded.dtype)
        .reshape((-1, 1, 1, 1))
    )
    ghost_low = jnp.flip(take_slab(padded, 3, 3, flux_axis), flux_axis) * flip_sign
    ghost_high = jnp.flip(take_slab(padded, cell_count, 3, flux_axis), flux_axis) * flip_sign
    low_side = jnp.where(at_first, ghost_low, take_slab(padded, 0, 3, flux_axis))
    high_side = jnp.where(at_last, ghost_high, take_slab(padded, cell_count + 3, 3, flux_axis))
    return jnp.concatenate(
        [low_side, take_slab(padded, 3, cell_count, flux_axis), high_side], axis=flux_axis
    )


def chem_rates(features, layer_one, layer_two, layer_three, layer_four):
    hidden_one = jax.nn.gelu(
        jnp.dot(layer_one, features, preferred_element_type=jnp.float32)
    ).astype(jnp.bfloat16)
    hidden_two = jax.nn.gelu(
        jnp.dot(layer_two, hidden_one, preferred_element_type=jnp.float32)
    ).astype(jnp.bfloat16)
    hidden_three = jax.nn.gelu(
        jnp.dot(layer_three, hidden_two, preferred_element_type=jnp.float32)
    ).astype(jnp.bfloat16)
    return jnp.dot(layer_four, hidden_three, preferred_element_type=jnp.float32).astype(
        jnp.bfloat16
    )


def body(fields, reacting, panel_map, layer_one, layer_two, layer_three, layer_four):
    recon_fields = to_recon(fields)
    gx_count = lax.axis_size("gx")
    gy_count = lax.axis_size("gy")
    gz_count = lax.axis_size("gz")
    at_first = (lax.axis_index("gx") == 0, lax.axis_index("gy") == 0, lax.axis_index("gz") == 0)
    at_last = (
        lax.axis_index("gx") == gx_count - 1,
        lax.axis_index("gy") == gy_count - 1,
        lax.axis_index("gz") == gz_count - 1,
    )
    padded = extended(recon_fields, (("gx", 1), ("gy", 2), ("gz", 3)), 3)
    line_fields = (padded[:, :, 3:-3, 3:-3], padded[:, 3:-3, :, 3:-3], padded[:, 3:-3, 3:-3, :])
    update = jnp.zeros_like(fields)
    push_low = None
    push_high = None
    for normal in range(3):
        line_block = mirror_walls(line_fields[normal], normal, at_first[normal], at_last[normal])
        face_fluxes = face_flux(line_block, normal)
        cell_count = face_fluxes.shape[normal + 1] - 1
        change = take_slab(face_fluxes, 1, cell_count, normal + 1) - take_slab(
            face_fluxes, 0, cell_count, normal + 1
        )
        update = update + change
        if normal == 1:
            push_low = face_fluxes[2, :, 0, :]
            push_high = face_fluxes[2, :, cell_count, :]
    cell_total = reacting.size
    react_flags = reacting.reshape(cell_total)
    capacity = BAL * min(4, gx_count)
    per_peer = capacity // gx_count
    row_rank = jnp.cumsum(react_flags) - 1
    slot_index = jnp.where(
        react_flags == 1, row_rank % gx_count * per_peer + row_rank // gx_count, capacity
    )
    flat_features = recon_fields.reshape(COMPS, cell_total).astype(jnp.bfloat16)
    packed = (
        jnp.zeros((COMPS, capacity), jnp.bfloat16).at[:, slot_index].set(flat_features, mode="drop")
    )
    rate_packed = chem_rates(packed, layer_one, layer_two, layer_three, layer_four)
    gathered = rate_packed[:, jnp.where(react_flags == 1, slot_index, 0)]
    source = jnp.where(react_flags[None, :] == 1, gathered.astype(jnp.float32), 0.0).reshape(
        fields.shape
    )
    new_fields = fields - TIME_STEP * update + CHEM_STEP * source
    on_low = lax.axis_index("gy") == 0
    on_high = lax.axis_index("gy") == gy_count - 1
    push_values = jnp.concatenate(
        [
            jnp.where(on_low, push_low, 0.0).reshape(-1),
            jnp.where(on_high, push_high, 0.0).reshape(-1),
        ]
    )
    panel_ids = jnp.concatenate([panel_map[0].reshape(-1), panel_map[1].reshape(-1)])
    panels_all = 2 * (fields.shape[1] * gx_count // PATCH) * (fields.shape[3] * gz_count // PATCH)
    own_panels = panels_all // (gx_count * gy_count * gz_count)
    partial_loads = jax.ops.segment_sum(push_values, panel_ids, num_segments=panels_all)
    totals = lax.psum(partial_loads, ("gx", "gy", "gz"))
    flat_index = (
        lax.axis_index("gx") * gy_count + lax.axis_index("gy")
    ) * gz_count + lax.axis_index("gz")
    result = lax.dynamic_slice_in_dim(totals, flat_index * own_panels, own_panels)
    impulse = result / float(PATCH * PATCH)
    return (new_fields, impulse)


def solution(mesh):
    return jax.shard_map(
        body,
        mesh=mesh,
        in_specs=(
            P(None, "gx", "gy", "gz"),
            P("gx", "gy", "gz"),
            P(None, "gx", "gz"),
            P(),
            P(),
            P(),
            P(),
        ),
        out_specs=(P(None, "gx", "gy", "gz"), P(("gx", "gy", "gz"))),
        check_vma=False,
    )
```

profile of v0, /device:TPU:1, one launch (start us, length us, event | category | flops | bytes accessed | tf_op | source)
XLA Modules:
  0.0 275.4 jit_solution(14904916895954684997)
XLA Ops:
  5.1 5.0 %collective-permute-start = (f32[12,3,8,128]{3,2,1,0:T(8,128)}, f32[12,3,8,128]{3,2,1,0:T(8,128)}, u32[]{:S(2)}, u32[]{:S(2)}) collective-permute-start(f32[12,3,8,128]{3,2,1,0:T(8,128)} %get-tuple-element.138), channel_id=1, source_target_pairs={{0,16},{16,32},{32,48},{48,64},{64,80},{80,96},{96,112},{112,128},... | collective-permute-start | bytes 442376 | tf_op jit(solution)/shard_map/ppermute | solution.py:24
  10.2 1.3 collective-permute-start.1
  16.4 2.7 copy.63
  21.6 21.7 %scatter_custom_fusion = bf16[12,256]{0,1:T(8,128)(2,1)} fusion(s32[8192]{0:T(1024)S(1)} %bitcast.214, bf16[8192,12]{1,0:T(8,128)(2,1)} %copy.63, bf16[]{:T(256)} %constant.78.clone.1), kind=kCustom, calls=%fused_computation.316 | custom fusion | bytes 6656 | tf_op jit(solution)/shard_map/scatter | solution.py:276
  43.3 3.2 %fusion.16 = bf16[800,256]{1,0:T(8,128)(2,1)} fusion(bf16[800,1600]{1,0:T(8,128)(2,1)S(1)} %copy-done, bf16[12,256]{0,1:T(8,128)(2,1)} %scatter_custom_fusion, bf16[1600,12]{0,1:T(8,128)(2,1)} %param.10), kind=kOutput, calls=%fused_computation.28 | convolution fusion | flops 670720000 | bytes 3014144 | tf_op jit(solution)/shard_map/dot_general | solution.py:229
  46.5 1.8 fusion.8
  48.8 1.8 rev.23
  50.6 1.8 rev.24
  52.4 1.9 rev.25
  55.4 29.4 %gather_fusion = bf16[8192,12]{1,0:T(8,128)(2,1)} fusion(bf16[12,256]{0,1:T(8,128)(2,1)S(1)} %copy.64, s32[8192]{0:T(1024)S(1)} %broadcast_clamp_fusion), kind=kCustom, calls=%fused_computation | custom fusion | bytes 425984 | tf_op jit(solution)/shard_map/gather | solution.py:279
  84.8 3.8 %convert_element_type.31 = f32[8192,12]{1,0:T(8,128)} convert(bf16[8192,12]{1,0:T(8,128)(2,1)} %gather_fusion) | non-fusion elementwise | flops 98304 | bytes 589824 | tf_op jit(solution)/shard_map/convert_element_type | solution.py:280
  88.6 3.6 %copy.66 = f32[12,8,8,128]{3,2,1,0:T(8,128)} copy(f32[12,8,8,128]{0,3,2,1:T(8,128)} %bitcast.175) | data formatting | bytes 786432 | tf_op jit(solution)/shard_map/convert_element_type | solution.py:280
  94.0 1.9 add_divide_fusion.2
  97.2 3.1 %collective-permute-start.2 = (f32[12,14,3,128]{3,1,2,0:T(8,128)S(1)}, f32[12,14,3,128]{3,1,2,0:T(8,128)S(1)}, u32[]{:S(2)}, u32[]{:S(2)}) collective-permute-start(f32[12,14,3,128]{3,1,2,0:T(8,128)S(1)} %copy.53), channel_id=1, source_target_pairs={{0,4},{4,8},{8,12},{1,5},{5,9},{9,13},{2,6},{6,10},{10,14},{3,7},{... | collective-permute-start | bytes 774152 | tf_op jit(solution)/shard_map/ppermute | solution.py:24
  100.4 1.5 collective-permute-start.3
  103.0 1.9 collective-permute-done.2
  105.1 3.7 %collective-permute-done.3 = f32[12,14,3,128]{3,1,2,0:T(8,128)S(1)} collective-permute-done((f32[12,14,3,128]{3,1,2,0:T(8,128)S(1)}, f32[12,14,3,128]{3,1,2,0:T(8,128)S(1)}, u32[]{:S(2)}, u32[]{:S(2)}) %collective-permute-start.3) | collective-permute-done | bytes 258080 | tf_op jit(solution)/shard_map/ppermute | solution.py:25
  109.9 3.6 %add_divide_fusion.1 = (f32[12,8,9,128]{3,2,1,0:T(8,128)S(1)}, f32[12,8,9,128]{3,2,1,0:T(8,128)S(1)}) fusion(f32[12,8,11,128]{3,2,1,0:T(8,128)S(1)} %get-tuple-element.130, f32[12,8,11,128]{3,2,1,0:T(8,128)S(1)} %get-tuple-element.131), kind=kLoop, calls=%fused_computation.80 | loop fusion | flops 13713408 | bytes 3538944 | tf_op jit(solution)/shard_map/div | solution.py:54
  116.2 13.9 %scatter_custom_fusion.1 = f32[4096]{0:T(1024)S(1)} fusion(s32[2048]{0:T(1024)} %pad_add_fusion, f32[2048]{0:T(1024)S(1)} %pad_maximum_fusion.9, f32[]{:T(128)} %constant.54.clone.1), kind=kCustom, calls=%fused_computation.342 | custom fusion | flops 2048 | bytes 16896 | tf_op jit(solution)/shard_map/scatter-add | solution.py:295
  130.2 111.1 %psum.7 = f32[4096]{0:T(1024)S(1)} all-reduce(f32[4096]{0:T(1024)S(1)} %scatter_custom_fusion.1), channel_id=1, replica_groups=mesh['gx'=32,'gy'=4,'gz'=4] {'gx','gy','gz'}, use_global_device_ids=true, to_apply=%region_11.12 | all-reduce | flops 4096 | bytes 32768 | tf_op jit(solution)/shard_map/psum | solution.py:296
  241.2 1.5 pad_maximum_fusion
  242.7 2.0 fusion.169
  244.7 3.4 %copy.59 = f32[12,14,14,3]{2,1,3,0:T(8,128)} copy(f32[12,14,14,3]{3,2,1,0:T(8,128)} %get-tuple-element.58) | data formatting | bytes 56448 | tf_op jit(solution)/shard_map/slice | solution.py:22
  248.1 2.1 collective-permute-start.4
  250.3 3.4 %copy.61 = f32[12,14,14,3]{2,1,3,0:T(8,128)} copy(f32[12,14,14,3]{3,2,1,0:T(8,128)} %get-tuple-element.57) | data formatting | bytes 56448 | tf_op jit(solution)/shard_map/slice | solution.py:23
  253.6 2.9 %collective-permute-start.5 = (f32[12,14,14,3]{2,1,3,0:T(8,128)}, f32[12,14,14,3]{2,1,3,0:T(8,128)}, u32[]{:S(2)}, u32[]{:S(2)}) collective-permute-start(f32[12,14,14,3]{2,1,3,0:T(8,128)} %copy.61), channel_id=1, source_target_pairs={{1,0},{2,1},{3,2},{5,4},{6,5},{7,6},{9,8},{10,9},{11,10},{13,12},{... | collective-permute-start | bytes 84680 | tf_op jit(solution)/shard_map/ppermute | solution.py:25
  257.1 1.7 slice.418
  258.8 2.3 copy.67
  262.0 1.7 slice.424
  263.7 2.3 copy.68
  266.0 1.5 multiply_select_fusion
  267.8 3.9 %add_divide_fusion = (f32[12,8,8,129]{3,2,1,0:T(8,128)S(1)}, f32[12,8,8,129]{3,2,1,0:T(8,128)S(1)}) fusion(f32[12,8,8,131]{3,2,1,0:T(8,128)S(1)} %get-tuple-element.134, f32[12,8,8,131]{3,2,1,0:T(8,128)S(1)} %get-tuple-element.135), kind=kLoop, calls=%fused_computation.53 | loop fusion | flops 12284928 | bytes 3170304 | tf_op jit(solution)/shard_map/div | solution.py:54
  (119 shorter events, 26.8 us)
Async XLA Ops:
  0.6 42.6 %copy-start = (bf16[800,1600]{1,0:T(8,128)(2,1)S(1)}, bf16[800,1600]{1,0:T(8,128)(2,1)}, u32[]{:S(2)}) copy-start(bf16[800,1600]{1,0:T(8,128)(2,1)} %param.11) | copy-start | bytes 7680004
  4.3 11.0 %copy-start.10 = (s32[2,8,128]{2,1,0:T(8,128)S(1)}, s32[2,8,128]{2,1,0:T(8,128)}, u32[]{:S(2)}) copy-start(s32[2,8,128]{2,1,0:T(8,128)} %param.9) | copy-start | bytes 24580
  5.1 87.6 %collective-permute-start = (f32[12,3,8,128]{3,2,1,0:T(8,128)}, f32[12,3,8,128]{3,2,1,0:T(8,128)}, u32[]{:S(2)}, u32[]{:S(2)}) collective-permute-start(f32[12,3,8,128]{3,2,1,0:T(8,128)} %get-tuple-element.138), channel_id=1, source_target_pairs={{0,16},{16,32},{32,48},{48,64},{64,80},{80,96},{96,112},{112,128},... | collective-permute-start | bytes 442376 | tf_op jit(solution)/shard_map/ppermute | solution.py:24
  10.2 82.6 %collective-permute-start.1 = (f32[12,3,8,128]{3,2,1,0:T(8,128)}, f32[12,3,8,128]{3,2,1,0:T(8,128)}, u32[]{:S(2)}, u32[]{:S(2)}) collective-permute-start(f32[12,3,8,128]{3,2,1,0:T(8,128)} %get-tuple-element.139), channel_id=1, source_target_pairs={{16,0},{32,16},{48,32},{64,48},{80,64},{96,80},{112,96},{128,112},... | collective-permute-start | bytes 442376 | tf_op jit(solution)/shard_map/ppermute | solution.py:25
  15.3 3.8 %copy-start.9 = (s32[8,8,128]{2,1,0:T(8,128)S(1)}, s32[8,8,128]{2,1,0:T(8,128)}, u32[]{:S(2)}) copy-start(s32[8,8,128]{2,1,0:T(8,128)} %param.8) | copy-start | bytes 98308
  43.3 3.2 %copy-start.16 = (bf16[12,400]{1,0:T(8,128)(2,1)S(1)}, bf16[12,400]{1,0:T(8,128)(2,1)}, u32[]{:S(2)}) copy-start(bf16[12,400]{1,0:T(8,128)(2,1)} %param.13) | copy-start | bytes 28804
  88.6 4.2 %copy-start.15 = (f32[12]{0:T(128)S(1)}, f32[12]{0:T(128)}, u32[]{:S(2)}) copy-start(f32[12]{0:T(128)} %compare_select_fusion.7) | copy-start | bytes 148
  97.2 7.7 %collective-permute-start.2 = (f32[12,14,3,128]{3,1,2,0:T(8,128)S(1)}, f32[12,14,3,128]{3,1,2,0:T(8,128)S(1)}, u32[]{:S(2)}, u32[]{:S(2)}) collective-permute-start(f32[12,14,3,128]{3,1,2,0:T(8,128)S(1)} %copy.53), channel_id=1, source_target_pairs={{0,4},{4,8},{8,12},{1,5},{5,9},{9,13},{2,6},{6,10},{10,14},{3,7},{... | collective-permute-start | bytes 774152 | tf_op jit(solution)/shard_map/ppermute | solution.py:24
  100.4 8.4 %collective-permute-start.3 = (f32[12,14,3,128]{3,1,2,0:T(8,128)S(1)}, f32[12,14,3,128]{3,1,2,0:T(8,128)S(1)}, u32[]{:S(2)}, u32[]{:S(2)}) collective-permute-start(f32[12,14,3,128]{3,1,2,0:T(8,128)S(1)} %copy.55), channel_id=1, source_target_pairs={{4,0},{8,4},{12,8},{5,1},{9,5},{13,9},{6,2},{10,6},{14,10},{7,3},{... | collective-permute-start | bytes 774152 | tf_op jit(solution)/shard_map/ppermute | solution.py:25
  102.0 0.7 copy-start.14
  102.7 6.2 %copy-start.7 = (f32[12,8,3,128]{3,2,1,0:T(4,128)S(1)}, f32[12,8,3,128]{3,2,1,0:T(4,128)}, u32[]{:S(2)}) copy-start(f32[12,8,3,128]{3,2,1,0:T(4,128)} %rev.23) | copy-start | bytes 442372
  102.7 6.2 %copy-start.8 = (f32[12,8,3,128]{3,2,1,0:T(4,128)S(1)}, f32[12,8,3,128]{3,2,1,0:T(4,128)}, u32[]{:S(2)}) copy-start(f32[12,8,3,128]{3,2,1,0:T(4,128)} %rev.24) | copy-start | bytes 442372
  105.0 4.1 %copy-start.3 = (f32[12,14,3,128]{3,2,1,0:T(4,128)}, f32[12,14,3,128]{3,2,1,0:T(4,128)S(1)}, u32[]{:S(2)}) copy-start(f32[12,14,3,128]{3,2,1,0:T(4,128)S(1)} %copy.54) | copy-start | bytes 774148
  109.0 0.7 copy-start.4
  114.0 0.7 copy-start.13
  115.3 0.9 copy-start.1
  248.1 9.0 %collective-permute-start.4 = (f32[12,14,14,3]{2,1,3,0:T(8,128)}, f32[12,14,14,3]{2,1,3,0:T(8,128)}, u32[]{:S(2)}, u32[]{:S(2)}) collective-permute-start(f32[12,14,14,3]{2,1,3,0:T(8,128)} %copy.59), channel_id=1, source_target_pairs={{0,1},{1,2},{2,3},{4,5},{5,6},{6,7},{8,9},{9,10},{10,11},{12,13},{... | collective-permute-start | bytes 84680 | tf_op jit(solution)/shard_map/ppermute | solution.py:24
  250.3 15.7 %copy-start.12 = (f32[12]{0:T(128)S(1)}, f32[12]{0:T(128)}, u32[]{:S(2)}) copy-start(f32[12]{0:T(128)} %compare_select_fusion.5) | copy-start | bytes 148
  253.6 8.3 %collective-permute-start.5 = (f32[12,14,14,3]{2,1,3,0:T(8,128)}, f32[12,14,14,3]{2,1,3,0:T(8,128)}, u32[]{:S(2)}, u32[]{:S(2)}) collective-permute-start(f32[12,14,14,3]{2,1,3,0:T(8,128)} %copy.61), channel_id=1, source_target_pairs={{1,0},{2,1},{3,2},{5,4},{6,5},{7,6},{9,8},{10,9},{11,10},{13,12},{... | collective-permute-start | bytes 84680 | tf_op jit(solution)/shard_map/ppermute | solution.py:25
  272.2 0.7 copy-start.11
  273.0 1.1 copy-start.2
  273.0 1.2 copy-start.5
  273.1 1.3 copy-start.6
where the time goes:
time: 276 us; the launch traced here: 275 us
  blocking collectives  111 us (40%)
  local copies, waits for them, and re-layouts  87.9 us (32%)
  other arithmetic  47.8 us (17%)
  starting transfers between devices  15.9 us (6%)
  waiting for transfers between devices  6.55 us (2%)
  matrix products  4.97 us (2%)
    psum x1, blocking collectives, body(): totals = lax.psum(partial_loads, ('gx', 'gy', 'gz'))  111 us
    gather x1, local copies, waits for them, and re-layouts, body(): gathered = rate_packed[:, jnp.where(react_flags == 1, slot_index, 0)]  29.4 us
    scatter x1, local copies, waits for them, and re-layouts, body(): jnp.zeros((COMPS, capacity), jnp.bfloat16).at[:, slot_index]  21.7 us
    scatter-add x1, other arithmetic, body(): jax.ops.segment_sum(push_values, panel_ids, num_segments=panels_all)  13.9 us
    ppermute x3, starting transfers between devices, extended(): before = lax.ppermute(last, axis, up)  10.3 us
    div x3, other arithmetic, weno_face(): (weight_zero * cand_zero + weight_one * cand_one + weight_two * cand_two)...  9.43 us
    unnamed x38, local copies, waits for them, and re-layouts  7.97 us
    ppermute x3, starting transfers between devices, extended(): after = lax.ppermute(initial, axis, down)  5.61 us
  transfers between devices with their start and end apart: 6, of which 3 were waited for; matrix products, arithmetic and copies ran while one was open for 33% of the time, Pallas kernels for 0%

commit v1 on v0

v1 whole, which is shorter than its diff:
```python
import functools
import math

import jax
import jax.numpy as jnp
from jax import lax
from jax.experimental import pallas as pl
from jax.experimental.pallas import tpu as pltpu
from jax.sharding import PartitionSpec as P

COMPS = 12
CX = 8
CY = 8
CZ = 128
ROWS = CX * CY
HALF = CZ // 2
CAP = 256
H1 = 1600
H2 = 800
H3 = 400
PATCH = 8
LANES = 128

TIME_STEP = 0.1
CHEM_STEP = 0.25
WENO_EPS = 1e-06
ALPHA = math.sqrt(12.0 / 13.0)
EPS_SCALED = WENO_EPS * 12.0 / 13.0
LOG_HEAT_HALF = 0.5 * math.log(1.4)

MESH = pl.DeviceIdType.MESH
F32 = jnp.float32
BF16 = jnp.bfloat16


def recip(x):
    r = pl.reciprocal(x, approx=True)
    return r * (2.0 - x * r)


def weno_pair(v):
    count = v.shape[0]
    d = v[1:] - v[:-1]
    q = d[1:] - d[:-1]
    g = (q[1:] - q[:-1]) * (1.0 / 3.0)
    da = d * ALPHA
    ha = q * (0.5 * ALPHA)
    qq = q * q + EPS_SCALED
    m = count - 4
    f0 = da[1 : 1 + m] + ha[0:m]
    f1 = da[1 : 1 + m] + ha[1 : 1 + m]
    f2 = da[2 : 2 + m] - ha[2 : 2 + m]
    t0 = f0 * f0 + qq[0:m]
    t1 = f1 * f1 + qq[1 : 1 + m]
    t2 = f2 * f2 + qq[2 : 2 + m]
    a = t1 * t2
    b = t0 * t2
    c = t0 * t1
    a = a * a
    b = b * b * 6.0
    c = c * c
    u = a + c + b
    x = a * g[0:m]
    y = c * g[1 : 1 + m]
    center = v[2 : 2 + m] + q[1 : 1 + m] * (1.0 / 3.0)
    hd = d * 0.5
    n = m - 1
    low = slice(0, n)
    high = slice(1, m)
    left = (
        center[low]
        + hd[1 : 1 + n]
        - (x[low] + 1.5 * y[low]) * pl.reciprocal(u[low] + 2.0 * c[low], approx=True)
    )
    right = (
        center[high]
        - hd[3 : 3 + n]
        + (y[high] + 1.5 * x[high]) * pl.reciprocal(u[high] + 2.0 * a[high], approx=True)
    )
    return left, right


def hllc(left, right, normal, only_push=False):
    rl = jnp.exp(left[0])
    rr = jnp.exp(right[0])
    p_l = jnp.exp(left[4])
    p_r = jnp.exp(right[4])
    cl = jnp.exp(0.5 * (left[4] - left[0]) + LOG_HEAT_HALF)
    cr = jnp.exp(0.5 * (right[4] - right[0]) + LOG_HEAT_HALF)
    ul = left[1 + normal]
    ur = right[1 + normal]
    sl = jnp.minimum(ul - cl, ur - cr)
    sr = jnp.maximum(ul + cl, ur + cr)
    al = rl * (sl - ul)
    ar = rr * (sr - ur)
    s = (p_r - p_l + al * ul - ar * ur) * recip(al - ar)
    take_left = jnp.maximum(s, sl) >= 0.0

    def pick(i, j):
        return jnp.where(take_left, i, j)

    rho = pick(rl, rr)
    p = pick(p_l, p_r)
    sk = pick(sl, sr)
    a = pick(al, ar)
    beyond = pick(sl, -sr) >= 0.0
    un = pick(ul, ur)
    inv = recip(sk - s)
    pstar = p + a * (s - un)
    u_face = jnp.where(beyond, un, s)
    p_face = jnp.where(beyond, p, pstar)
    mass = jnp.where(beyond, rho, a * inv) * u_face
    push = mass * u_face + p_face
    if only_push:
        return push
    vel = [un if i == normal else pick(left[1 + i], right[1 + i]) for i in range(3)]
    energy = 2.5 * p + 0.5 * rho * (vel[0] * vel[0] + vel[1] * vel[1] + vel[2] * vel[2])
    estar = ((sk - un) * energy + pstar * s - p * un) * inv
    e_face = jnp.where(beyond, energy, estar)
    flux = [mass]
    for i in range(3):
        flux.append(push if i == normal else mass * vel[i])
    flux.append(u_face * (e_face + p_face))
    for i in range(5, COMPS):
        flux.append(mass * pick(left[i], right[i]))
    return flux


def gelu(x):
    k = math.sqrt(2.0 / math.pi)
    y = x * (x * x * (0.044715 * k) + k)
    h = 0.5 * x
    return h * jnp.tanh(y) + h


def dot_nt(a, b):
    return lax.dot_general(a, b, (((1,), (1,)), ((), ())), preferred_element_type=F32)


def dot_tn(a, b):
    return lax.dot_general(a, b, (((0,), (0,)), ((), ())), preferred_element_type=F32)


def iota(shape, dim):
    return lax.broadcasted_iota(jnp.int32, shape, dim)


def one_where(mask):
    return jnp.where(mask, 1.0, 0.0)


def kernel(
    sizes,
    fields_hbm,
    react_hbm,
    pmap_hbm,
    w1_hbm,
    w2_hbm,
    w3_hbm,
    w4_hbm,
    out_ref,
    imp_ref,
    fields,
    react,
    pmap,
    w1,
    w2,
    w3,
    w4,
    rec,
    ybuf,
    zbuf,
    xlo,
    xhi,
    ylo,
    yhi,
    zlo,
    zhi,
    st_l,
    st_r,
    flux_x,
    flux_y,
    flux_z,
    turn_y,
    turn_z,
    hid1,
    hid2,
    source,
    contrib,
    rows1,
    parts,
    own,
    load_sem,
    send_sem,
    recv_sem,
    s1_send,
    s1_recv,
    s2_send,
    s2_recv,
):
    nx, ny, nz = sizes
    gx = lax.axis_index("gx")
    gy = lax.axis_index("gy")
    gz = lax.axis_index("gz")
    is_wall = (gy == 0) | (gy == ny - 1)
    group = ny * nz
    me = gy * nz + gz
    walls = 2 * nz

    loads = []
    for i, (src, dst) in enumerate(
        (
            (fields_hbm, fields),
            (react_hbm, react),
            (pmap_hbm, pmap),
            (w1_hbm, w1),
            (w2_hbm, w2),
            (w3_hbm, w3),
            (w4_hbm, w4),
        )
    ):
        copy = pltpu.make_async_copy(src, dst, load_sem.at[i])
        copy.start()
        loads.append(copy)

    barrier = pltpu.get_barrier_semaphore()
    around = {
        "xlo": {"gx": lax.rem(gx + nx - 1, nx)},
        "xhi": {"gx": lax.rem(gx + 1, nx)},
        "ylo": {"gy": lax.rem(gy + ny - 1, ny)},
        "yhi": {"gy": lax.rem(gy + 1, ny)},
        "zlo": {"gz": lax.rem(gz + nz - 1, nz)},
        "zhi": {"gz": lax.rem(gz + 1, nz)},
    }
    for where in around.values():
        pl.semaphore_signal(barrier, inc=1, device_id=where, device_id_type=MESH)

    def greet_wall(w, carry):
        to_y = (w // nz) * (ny - 1)
        to_z = lax.rem(w, nz)

        @pl.when(to_y * nz + to_z != me)
        def _():
            pl.semaphore_signal(
                barrier, inc=1, device_id={"gy": to_y, "gz": to_z}, device_id_type=MESH
            )

        return carry

    lax.fori_loop(0, walls, greet_wall, 0)

    @pl.when(is_wall)
    def _():
        def greet_row(j, carry):
            pl.semaphore_signal(
                barrier, inc=1, device_id={"gx": lax.rem(gx + j, nx)}, device_id_type=MESH
            )
            return carry

        lax.fori_loop(1, nx, greet_row, 0)

    loads[0].wait()

    def recon_step(i, carry):
        span = pl.ds(pl.multiple_of(i * 16, 16), 16)
        rho = fields[0, span, :]
        inv = recip(rho)
        inv = inv * (2.0 - rho * inv)
        vel = [fields[k, span, :] * inv for k in (1, 2, 3)]
        speed = vel[0] * vel[0] + vel[1] * vel[1] + vel[2] * vel[2]
        pressure = 0.4 * (fields[4, span, :] - 0.5 * rho * speed)
        rec[0, span, :] = jnp.log(rho)
        for k in range(3):
            rec[1 + k, span, :] = vel[k]
        rec[4, span, :] = jnp.log(pressure)
        for k in range(5, COMPS):
            rec[k, span, :] = fields[k, span, :] * inv
        return carry

    lax.fori_loop(0, ROWS // 16, recon_step, 0)

    @pl.when(is_wall)
    def _():
        pl.semaphore_wait(barrier, 6 + nx - 1 + group - 1)

    @pl.when(jnp.logical_not(is_wall))
    def _():
        pl.semaphore_wait(barrier, 6)

    sends = []

    def send(i, src, dst, where):
        copy = pltpu.make_async_remote_copy(
            src_ref=src,
            dst_ref=dst,
            send_sem=send_sem.at[i],
            recv_sem=recv_sem.at[i],
            device_id=around[where],
            device_id_type=MESH,
        )
        copy.start()
        sends.append(copy)

    send(0, rec.at[:, pl.ds(0, 24), :], xhi, "xlo")
    send(1, rec.at[:, pl.ds(ROWS - 24, 24), :], xlo, "xhi")

    def turn_to_y(k, carry):
        for y in range(CY):
            ybuf[k, pl.ds(8 * y, 8), :] = rec[k, pl.ds(y, CX, stride=CY), :]
        return carry

    lax.fori_loop(0, COMPS, turn_to_y, 0)
    send(2, ybuf.at[:, pl.ds(0, 24), :], yhi, "ylo")
    send(3, ybuf.at[:, pl.ds(ROWS - 24, 24), :], ylo, "yhi")

    first_half = iota((HALF, LANES), 1) < HALF

    def turn_to_z(i, carry):
        both = rec[pl.ds(2 * i, 2), :, :].reshape(2 * ROWS, CZ).T
        top = both[:HALF]
        bottom = both[HALF:]
        zbuf[2 * i, pl.ds(8, HALF), :] = jnp.where(first_half, top, pltpu.roll(bottom, HALF, 1))
        zbuf[2 * i + 1, pl.ds(8, HALF), :] = jnp.where(first_half, pltpu.roll(top, HALF, 1), bottom)
        return carry

    lax.fori_loop(0, COMPS // 2, turn_to_z, 0)
    send(4, zbuf.at[:, pl.ds(8, 8), :], zhi, "zlo")
    send(5, zbuf.at[:, pl.ds(HALF, 8), :], zlo, "zhi")

    loads[2].wait()

    @pl.when(is_wall)
    def _():
        low = gy == 0

        def line(k, sign):
            near = [
                jnp.where(low, ybuf[k, pl.ds(8 * j, 8), :], ybuf[k, pl.ds(ROWS - 8 - 8 * j, 8), :])
                for j in range(3)
            ]
            ghost = [sign * x for x in near]
            below = ghost[::-1] + near
            above = near[::-1] + ghost
            return jnp.stack([jnp.where(low, i, j) for i, j in zip(below, above)])

        left, right = {}, {}
        for k in (0, 2, 4):
            left[k], right[k] = weno_pair(line(k, -1.0 if k == 2 else 1.0))
        push = hllc(left, right, 1, only_push=True)[0] * (1.0 / (PATCH * PATCH))
        ids = jnp.where(low, pmap[0], pmap[1])
        total = jnp.zeros((nx, LANES), F32)
        for h in range(2):
            value = jnp.sum(push[4 * h : 4 * h + 4], axis=0, keepdims=True)
            panel = ids[4 * h : 4 * h + 1]
            spread = jnp.where(iota((nx, LANES), 0) == panel // LANES, value, 0.0)
            lane = one_where(iota((LANES, LANES), 0) == panel % LANES).astype(BF16)
            big = spread.astype(BF16)
            small = (spread - big.astype(F32)).astype(BF16)
            total = total + dot_nt(big, lane) + dot_nt(small, lane)
        contrib[...] = total.reshape(nx, 1, LANES)
        rows1[0] = contrib[gx]

        def send_row(j, carry):
            to = lax.rem(gx + j, nx)
            pltpu.make_async_remote_copy(
                src_ref=contrib.at[to],
                dst_ref=rows1.at[j],
                send_sem=s1_send,
                recv_sem=s1_recv,
                device_id={"gx": to},
                device_id_type=MESH,
            ).start()
            return carry

        lax.fori_loop(1, nx, send_row, 0)

    loads[1].wait()
    hot = react[...] > 0
    flags = one_where(hot).astype(BF16)
    upto = one_where(iota((CZ, CZ), 0) <= iota((CZ, CZ), 1)).astype(BF16)
    within = jnp.dot(flags, upto, preferred_element_type=F32)
    sums = jnp.dot(flags, jnp.ones((CZ, CAP), BF16), preferred_element_type=F32)
    above = one_where(iota((ROWS, ROWS), 1) < iota((ROWS, ROWS), 0)).astype(BF16)
    start = jnp.dot(above, sums.astype(BF16), preferred_element_type=F32)
    slot = iota((ROWS, CAP), 1).astype(F32)
    row_hot = one_where((start <= slot) & (slot < start + sums))
    rank = jnp.where(hot, start[:, :CZ] + within, 0.0).astype(BF16)
    sums_t = dot_nt(jnp.ones((CAP, CZ), BF16), flags)
    before = one_where(iota((ROWS, ROWS), 0) < iota((ROWS, ROWS), 1)).astype(BF16)
    start_t = jnp.dot(sums_t.astype(BF16), before, preferred_element_type=F32)
    slot_t = iota((CAP, ROWS), 0).astype(F32)
    row_hot_t = one_where((start_t <= slot_t) & (slot_t < start_t + sums_t)).astype(BF16)
    line_rank = jnp.dot(row_hot_t, rank, preferred_element_type=F32)
    lane_hot = one_where(line_rank == iota((CAP, CZ), 0).astype(F32) + 1.0).astype(BF16)

    cells = rec[...].reshape(COMPS * ROWS, CZ).astype(BF16)
    spread_cells = dot_nt(cells, lane_hot).reshape(COMPS, ROWS, CAP)
    features = jnp.sum(spread_cells * row_hot[None], axis=1).astype(BF16)

    loads[3].wait()
    hid1[...] = gelu(dot_tn(w1[...], features)).astype(BF16)
    loads[4].wait()
    hid2[...] = gelu(jnp.dot(w2[...], hid1[...], preferred_element_type=F32)).astype(BF16)
    loads[5].wait()
    loads[6].wait()
    hid3 = gelu(jnp.dot(w3[...], hid2[...], preferred_element_type=F32)).astype(BF16)
    rates = jnp.dot(w4[...], hid3, preferred_element_type=F32).astype(BF16).astype(F32)
    spread_rates = (rates[:, None, :] * row_hot[None]).reshape(COMPS * ROWS, CAP).astype(BF16)
    source[...] = jnp.dot(spread_rates, lane_hot, preferred_element_type=F32).reshape(
        COMPS, ROWS, CZ
    )

    slot_of = (gy // jnp.int32(max(ny - 1, 1))) * nz + gz

    @pl.when(is_wall)
    def _():
        pltpu.make_async_copy(rows1.at[pl.ds(1, nx - 1)], rows1.at[pl.ds(1, nx - 1)], s1_recv).wait()
        own[...] = jnp.sum(rows1[...], axis=0)
        parts[slot_of] = own[...]

        def send_part(j, carry):
            to = lax.rem(me + j, group)
            pltpu.make_async_remote_copy(
                src_ref=own,
                dst_ref=parts.at[slot_of],
                send_sem=s2_send,
                recv_sem=s2_recv,
                device_id={"gy": to // nz, "gz": lax.rem(to, nz)},
                device_id_type=MESH,
            ).start()
            return carry

        lax.fori_loop(1, group, send_part, 0)

    def faces(load, normal, flux):
        def weno_step(k, carry):
            left, right = weno_pair(load(k))
            st_l[k] = left
            st_r[k] = right
            return carry

        lax.fori_loop(0, COMPS, weno_step, 0)

        def flux_step(i, carry):
            span = pl.ds(i * 3, 3)
            left = [st_l[k, span] for k in range(COMPS)]
            right = [st_r[k, span] for k in range(COMPS)]
            for k, x in enumerate(hllc(left, right, normal)):
                flux[k, span] = x
            return carry

        lax.fori_loop(0, 3, flux_step, 0)

    def sign_of(k, normal):
        return jnp.where(k == 1 + normal, -1.0, 1.0).astype(F32)

    sends[4].wait_recv()
    sends[5].wait_recv()
    first_lanes = iota((8, LANES), 1) < HALF

    def ghosts_z(k, carry):
        zbuf[k, pl.ds(0, 8), :] = pltpu.roll(
            jnp.where(first_lanes, zbuf[k, pl.ds(HALF, 8), :], zlo[k]), HALF, 1
        )
        zbuf[k, pl.ds(HALF + 8, 8), :] = pltpu.roll(
            jnp.where(first_lanes, zhi[k], zbuf[k, pl.ds(8, 8), :]), HALF, 1
        )
        return carry

    lax.fori_loop(0, COMPS, ghosts_z, 0)
    lane_low = iota((1, LANES), 1) < HALF

    @pl.when(gz == 0)
    def _():
        def mirror(k, carry):
            for j in range(3):
                here = zbuf[k, pl.ds(7 - j, 1), :]
                inside = zbuf[k, pl.ds(8 + j, 1), :] * sign_of(k, 2)
                zbuf[k, pl.ds(7 - j, 1), :] = jnp.where(lane_low, inside, here)
            return carry

        lax.fori_loop(0, COMPS, mirror, 0)

    @pl.when(gz == nz - 1)
    def _():
        def mirror(k, carry):
            for j in range(3):
                here = zbuf[k, pl.ds(HALF + 8 + j, 1), :]
                inside = zbuf[k, pl.ds(HALF + 7 - j, 1), :] * sign_of(k, 2)
                zbuf[k, pl.ds(HALF + 8 + j, 1), :] = jnp.where(lane_low, here, inside)
            return carry

        lax.fori_loop(0, COMPS, mirror, 0)

    faces(
        lambda k: jnp.stack([zbuf[k, pl.ds(5 + j, 8, stride=8), :] for j in range(14)]), 2, flux_z
    )

    def mirror_planes(inner, low, high, normal, place, count):
        @pl.when(place == 0)
        def _():
            def mirror(k, carry):
                for j in range(3):
                    low[k, pl.ds(16 - 8 * j, 8), :] = inner[k, pl.ds(8 * j, 8), :] * sign_of(k, normal)
                return carry

            lax.fori_loop(0, COMPS, mirror, 0)

        @pl.when(place == count - 1)
        def _():
            def mirror(k, carry):
                for j in range(3):
                    high[k, pl.ds(8 * j, 8), :] = inner[k, pl.ds(ROWS - 8 - 8 * j, 8), :] * sign_of(
                        k, normal
                    )
                return carry

            lax.fori_loop(0, COMPS, mirror, 0)

    def planes(low, inner, high):
        def load(k):
            return jnp.concatenate(
                [low[k].reshape(3, 8, CZ), inner[k].reshape(8, 8, CZ), high[k].reshape(3, 8, CZ)]
            )

        return load

    sends[2].wait_recv()
    sends[3].wait_recv()
    mirror_planes(ybuf, ylo, yhi, 1, gy, ny)
    faces(planes(ylo, ybuf, yhi), 1, flux_y)
    sends[0].wait_recv()
    sends[1].wait_recv()
    mirror_planes(rec, xlo, xhi, 0, gx, nx)
    faces(planes(xlo, rec, xhi), 0, flux_x)

    def finish(i, carry):
        change = []
        for h in range(2):
            k = 2 * i + h
            along_z = flux_z[k, pl.ds(1, 8)] - flux_z[k, pl.ds(0, 8)]
            along_y = flux_y[k, pl.ds(1, 8)] - flux_y[k, pl.ds(0, 8)]
            for j in range(8):
                turn_z[h, pl.ds(j, 8, stride=8), :] = along_z[j]
                turn_y[h, pl.ds(j, 8, stride=8), :] = along_y[j]
            change.append((flux_x[k, pl.ds(1, 8)] - flux_x[k, pl.ds(0, 8)]).reshape(ROWS, CZ))
        one = turn_z[0]
        two = turn_z[1]
        top = jnp.where(first_half, one, pltpu.roll(two, HALF, 1))
        bottom = jnp.where(first_half, pltpu.roll(one, HALF, 1), two)
        back = jnp.concatenate([top, bottom], axis=0).T
        for h in range(2):
            k = 2 * i + h
            whole = change[h] + turn_y[h] + back[ROWS * h : ROWS * h + ROWS]
            out_ref[k] = fields[k] - TIME_STEP * whole + CHEM_STEP * source[k]
        return carry

    lax.fori_loop(0, COMPS // 2, finish, 0)

    @pl.when(is_wall)
    def _():
        few = pl.ds(0, walls - 1)
        pltpu.make_async_copy(parts.at[few], parts.at[few], s2_recv).wait()
        many = pl.ds(1, nx - 1)
        pltpu.make_async_copy(contrib.at[many], contrib.at[many], s1_send).wait()

        def sent(j, carry):
            pltpu.make_async_copy(own, own, s2_send).wait()
            return carry

        lax.fori_loop(1, group, sent, 0)

    @pl.when(jnp.logical_not(is_wall))
    def _():
        pltpu.make_async_copy(parts, parts, s2_recv).wait()

    total = jnp.sum(parts[...], axis=0)
    mine = LANES // group
    wide = jnp.broadcast_to(total, (8, LANES))
    imp_ref[...] = pltpu.roll(wide, lax.rem(LANES - me * mine, LANES), 1)
    for copy in sends:
        copy.wait_send()


def body(fields, reacting, panel_map, layer_one, layer_two, layer_three, layer_four):
    sizes = (lax.axis_size("gx"), lax.axis_size("gy"), lax.axis_size("gz"))
    nx, ny, nz = sizes
    any_spec = pl.BlockSpec(memory_space=pl.ANY)
    vmem_spec = pl.BlockSpec(memory_space=pltpu.VMEM)
    plane = (COMPS, ROWS, CZ)
    ghost = (COMPS, 24, CZ)
    state = (COMPS, 9, 8, CZ)
    dma = pltpu.SemaphoreType.DMA
    new_fields, impulse = pl.pallas_call(
        functools.partial(kernel, sizes),
        out_shape=(
            jax.ShapeDtypeStruct(plane, F32),
            jax.ShapeDtypeStruct((8, LANES), F32),
        ),
        in_specs=[any_spec] * 7,
        out_specs=(vmem_spec, vmem_spec),
        scratch_shapes=[
            pltpu.VMEM(plane, F32),
            pltpu.VMEM((ROWS, CZ), jnp.int32),
            pltpu.VMEM((2, CX, CZ), jnp.int32),
            pltpu.VMEM((COMPS, H1), BF16),
            pltpu.VMEM((H2, H1), BF16),
            pltpu.VMEM((H3, H2), BF16),
            pltpu.VMEM((COMPS, H3), BF16),
            pltpu.VMEM(plane, F32),
            pltpu.VMEM(plane, F32),
            pltpu.VMEM((COMPS, HALF + 16, LANES), F32),
            pltpu.VMEM(ghost, F32),
            pltpu.VMEM(ghost, F32),
            pltpu.VMEM(ghost, F32),
            pltpu.VMEM(ghost, F32),
            pltpu.VMEM((COMPS, 8, LANES), F32),
            pltpu.VMEM((COMPS, 8, LANES), F32),
            pltpu.VMEM(state, F32),
            pltpu.VMEM(state, F32),
            pltpu.VMEM(state, F32),
            pltpu.VMEM(state, F32),
            pltpu.VMEM(state, F32),
            pltpu.VMEM((2, ROWS, CZ), F32),
            pltpu.VMEM((2, ROWS, CZ), F32),
            pltpu.VMEM((H1, CAP), BF16),
            pltpu.VMEM((H2, CAP), BF16),
            pltpu.VMEM(plane, F32),
            pltpu.VMEM((nx, 1, LANES), F32),
            pltpu.VMEM((nx, 1, LANES), F32),
            pltpu.VMEM((2 * nz, 1, LANES), F32),
            pltpu.VMEM((1, LANES), F32),
            dma((7,)),
            dma((6,)),
            dma((6,)),
            dma(()),
            dma(()),
            dma(()),
            dma(()),
        ],
        compiler_params=pltpu.CompilerParams(
            collective_id=0, has_side_effects=True, vmem_limit_bytes=48 * 2**20
        ),
    )(
        fields.reshape(plane),
        reacting.reshape(ROWS, CZ),
        panel_map,
        layer_one.T,
        layer_two,
        layer_three,
        layer_four,
    )
    own_panels = 2 * nx * nz * (CZ // PATCH) // (nx * ny * nz)
    return new_fields.reshape(fields.shape), impulse[0, :own_panels]


def solution(mesh):
    return jax.shard_map(
        body,
        mesh=mesh,
        in_specs=(
            P(None, "gx", "gy", "gz"),
            P("gx", "gy", "gz"),
            P(None, "gx", "gz"),
            P(),
            P(),
            P(),
            P(),
        ),
        out_specs=(P(None, "gx", "gy", "gz"), P(("gx", "gy", "gz"))),
        check_vma=False,
    )
```

time: 276 us -> 41.8 us (0.15)
  blocking collectives: 111 us -> 0 us
  local copies, waits for them, and re-layouts: 87.9 us -> 8.09 us
  other arithmetic: 47.8 us -> 0 us
  Pallas kernels: 0 us -> 32.4 us
  starting transfers between devices: 15.9 us -> 0 us
  waiting for transfers between devices: 6.55 us -> 0 us
  matrix products: 4.97 us -> 0 us
    psum x1 -> x0, blocking collectives: 111 us -> none  [body(): totals = lax.psum(partial_loads, ('gx', 'gy', 'gz'))]
    pallas_call x0 -> x1, Pallas kernels: none -> 32.4 us  [body(): pl.pallas_call(functools.partial(kernel, sizes), out_shape=(jax.ShapeDtyp...]
    gather x1 -> x0, local copies, waits for them, and re-layouts: 29.4 us -> none  [body(): gathered = rate_packed[:, jnp.where(react_flags == 1, slot_index, 0)]]
    scatter x1 -> x0, local copies, waits for them, and re-layouts: 21.7 us -> none  [body(): jnp.zeros((COMPS, capacity), jnp.bfloat16).at[:, slot_index]]
    ppermute x6 -> x0, starting transfers between devices: 15.9 us -> none  [the longest x3 10.3 us: extended(): before = lax.ppermute(last, axis, up)]
    slice x12 -> x0, local copies, waits for them, and re-layouts: 15.6 us -> none  [the longest x3 5.4 us: extended(): initial = lax.slice_in_dim(array, 0, width, axis=dim)]
    scatter-add x1 -> x0, other arithmetic: 13.9 us -> none  [body(): jax.ops.segment_sum(push_values, panel_ids, num_segments=panels_all)]
    div x4 -> x0, other arithmetic: 10 us -> none  [the longest x3 9.43 us: weno_face(): (weight_zero * cand_zero + weight_one * cand_one + weight_two * cand_two)...]
  transfers between devices with their start and end apart: 6 -> 0, of which waited for: 3 -> 0; matrix products, arithmetic and copies ran while one was open for 33% -> 0% of each run, Pallas kernels for 0% -> 0%
where the time goes in v1:
time: 41.8 us; the launch traced here: 41.1 us
  Pallas kernels  32.4 us (78%)
  local copies, waits for them, and re-layouts  8.09 us (19%)
  between operations  0.66 us (2%)
    pallas_call x1, Pallas kernels, body(): pl.pallas_call(functools.partial(kernel, sizes), out_shape=(jax.ShapeDtyp...  32.4 us
    unnamed x15, local copies, waits for them, and re-layouts  7.57 us

profile of v1, /device:TPU:1, one launch (start us, length us, event | category | flops | bytes accessed | tf_op | source)
XLA Modules:
  0.0 41.1 jit_solution(8315321663674045563)
XLA Ops:
  0.6 0.0 copy-start
  0.6 1.7 %copy-done = bf16[800,1600]{1,0:T(8,128)(2,1)S(1)} copy-done((bf16[800,1600]{1,0:T(8,128)(2,1)S(1)}, bf16[800,1600]{1,0:T(8,128)(2,1)}, u32[]{:S(2)}) %copy-start) | copy-done | bytes 2560024
  2.4 0.0 copy-start.1
  2.4 1.1 %copy-done.1 = bf16[400,800]{1,0:T(8,128)(2,1)S(1)} copy-done((bf16[400,800]{1,0:T(8,128)(2,1)S(1)}, bf16[400,800]{1,0:T(8,128)(2,1)}, u32[]{:S(2)}) %copy-start.1) | copy-done | bytes 640024
  3.5 0.0 copy-start.2
  3.5 1.0 %copy-done.2 = f32[12,8,8,128]{3,2,1,0:T(8,128)S(1)} copy-done((f32[12,8,8,128]{3,2,1,0:T(8,128)S(1)}, f32[12,8,8,128]{3,2,1,0:T(8,128)}, u32[]{:S(2)}) %copy-start.2) | copy-done | bytes 393240
  4.5 0.0 copy-start.3
  4.5 0.8 %copy-done.3 = bf16[1600,12]{0,1:T(8,128)(2,1)S(1)} copy-done((bf16[1600,12]{0,1:T(8,128)(2,1)S(1)}, bf16[1600,12]{0,1:T(8,128)(2,1)}, u32[]{:S(2)}) %copy-start.3) | copy-done | bytes 38424
  5.3 0.0 copy-start.4
  5.3 0.8 %copy-done.4 = s32[8,8,128]{2,1,0:T(8,128)S(1)} copy-done((s32[8,8,128]{2,1,0:T(8,128)S(1)}, s32[8,8,128]{2,1,0:T(8,128)}, u32[]{:S(2)}) %copy-start.4) | copy-done | bytes 32792
  6.1 0.0 copy-start.5
  6.1 0.7 %copy-done.5 = bf16[12,400]{1,0:T(8,128)(2,1)S(1)} copy-done((bf16[12,400]{1,0:T(8,128)(2,1)S(1)}, bf16[12,400]{1,0:T(8,128)(2,1)}, u32[]{:S(2)}) %copy-start.5) | copy-done | bytes 9624
  6.8 0.0 copy-start.6
  6.8 0.7 %copy-done.6 = s32[2,8,128]{2,1,0:T(8,128)S(1)} copy-done((s32[2,8,128]{2,1,0:T(8,128)S(1)}, s32[2,8,128]{2,1,0:T(8,128)}, u32[]{:S(2)}) %copy-start.6) | copy-done | bytes 8216
  7.5 32.4 %shard_map.86 = (f32[12,64,128]{2,1,0:T(8,128)S(1)}, f32[8,128]{1,0:T(8,128)S(1)}) custom-call(f32[12,64,128]{2,1,0:T(8,128)S(1)} %bitcast.6, s32[64,128]{1,0:T(8,128)S(1)} %bitcast.9, s32[2,8,128]{2,1,0:T(8,128)S(1)} %copy-done.6, bf16[12,1600]{1,0:T(8,128)(2,1)S(1)} %bitcast.8, bf16[800,1600]{1,0:T(8,128)(2,1)S(1)} %copy-done, ...), custom_call_target="tpu_custom_call" | custom-call | tf_op jit(solution)/shard_map/pallas_call | solution.py:594
  39.9 0.5 %slice_bitcast_fusion = f32[8]{0:T(128)} fusion(f32[8,128]{1,0:T(8,128)S(1)} %get-tuple-element.5), kind=kLoop, calls=%fused_computation | loop fusion | bytes 64 | tf_op jit(solution)/shard_map/squeeze | solution.py:654
  40.4 0.7 %copy.10 = f32[12,8,8,128]{3,2,1,0:T(8,128)} copy(f32[12,8,8,128]{3,2,1,0:T(8,128)S(1)} %bitcast.7) | data formatting | bytes 786432
Async XLA Ops:
  0.6 1.8 %copy-start = (bf16[800,1600]{1,0:T(8,128)(2,1)S(1)}, bf16[800,1600]{1,0:T(8,128)(2,1)}, u32[]{:S(2)}) copy-start(bf16[800,1600]{1,0:T(8,128)(2,1)} %w2_hbm.1) | copy-start | bytes 7680004
  2.4 1.1 %copy-start.1 = (bf16[400,800]{1,0:T(8,128)(2,1)S(1)}, bf16[400,800]{1,0:T(8,128)(2,1)}, u32[]{:S(2)}) copy-start(bf16[400,800]{1,0:T(8,128)(2,1)} %w3_hbm.1) | copy-start | bytes 1920004
  3.5 1.0 %copy-start.2 = (f32[12,8,8,128]{3,2,1,0:T(8,128)S(1)}, f32[12,8,8,128]{3,2,1,0:T(8,128)}, u32[]{:S(2)}) copy-start(f32[12,8,8,128]{3,2,1,0:T(8,128)} %param.7) | copy-start | bytes 1179652
  4.5 0.8 %copy-start.3 = (bf16[1600,12]{0,1:T(8,128)(2,1)S(1)}, bf16[1600,12]{0,1:T(8,128)(2,1)}, u32[]{:S(2)}) copy-start(bf16[1600,12]{0,1:T(8,128)(2,1)} %param.10) | copy-start | bytes 115204
  5.3 0.8 %copy-start.4 = (s32[8,8,128]{2,1,0:T(8,128)S(1)}, s32[8,8,128]{2,1,0:T(8,128)}, u32[]{:S(2)}) copy-start(s32[8,8,128]{2,1,0:T(8,128)} %param.8) | copy-start | bytes 98308
  6.1 0.7 %copy-start.5 = (bf16[12,400]{1,0:T(8,128)(2,1)S(1)}, bf16[12,400]{1,0:T(8,128)(2,1)}, u32[]{:S(2)}) copy-start(bf16[12,400]{1,0:T(8,128)(2,1)} %w4_hbm.1) | copy-start | bytes 28804
  6.8 0.7 %copy-start.6 = (s32[2,8,128]{2,1,0:T(8,128)S(1)}, s32[2,8,128]{2,1,0:T(8,128)}, u32[]{:S(2)}) copy-start(s32[2,8,128]{2,1,0:T(8,128)} %pmap_hbm.1) | copy-start | bytes 24580

commit v2 on v1

--- a/solution.py
+++ b/solution.py
@@ -197,6 +197,7 @@
     s1_recv,
     s2_send,
     s2_recv,
+    ready,
 ):
     nx, ny, nz = sizes
     gx = lax.axis_index("gx")
@@ -249,15 +250,19 @@
 
     lax.fori_loop(0, walls, greet_wall, 0)
 
+    half = nx // 2
+    rank = lax.rem(gx, half) * 2 + gx // half
+
+    def ranked(r):
+        return lax.rem(r, 2) * half + r // 2
+
     @pl.when(is_wall)
     def _():
-        def greet_row(j, carry):
-            pl.semaphore_signal(
-                barrier, inc=1, device_id={"gx": lax.rem(gx + j, nx)}, device_id_type=MESH
-            )
-            return carry
-
-        lax.fori_loop(1, nx, greet_row, 0)
+        def greet_row(r, carry):
+            pl.semaphore_signal(barrier, inc=1, device_id={"gx": ranked(r)}, device_id_type=MESH)
+            return carry
+
+        lax.fori_loop(rank + 1, nx, greet_row, 0)
 
     loads[0].wait()
 
@@ -281,7 +286,7 @@
 
     @pl.when(is_wall)
     def _():
-        pl.semaphore_wait(barrier, 6 + nx - 1 + group - 1)
+        pl.semaphore_wait(barrier, 6 + rank + group - 1)
 
     @pl.when(jnp.logical_not(is_wall))
     def _():
@@ -304,28 +309,17 @@
     send(0, rec.at[:, pl.ds(0, 24), :], xhi, "xlo")
     send(1, rec.at[:, pl.ds(ROWS - 24, 24), :], xlo, "xhi")
 
-    def turn_to_y(k, carry):
-        for y in range(CY):
-            ybuf[k, pl.ds(8 * y, 8), :] = rec[k, pl.ds(y, CX, stride=CY), :]
-        return carry
-
-    lax.fori_loop(0, COMPS, turn_to_y, 0)
-    send(2, ybuf.at[:, pl.ds(0, 24), :], yhi, "ylo")
-    send(3, ybuf.at[:, pl.ds(ROWS - 24, 24), :], ylo, "yhi")
-
-    first_half = iota((HALF, LANES), 1) < HALF
-
-    def turn_to_z(i, carry):
-        both = rec[pl.ds(2 * i, 2), :, :].reshape(2 * ROWS, CZ).T
-        top = both[:HALF]
-        bottom = both[HALF:]
-        zbuf[2 * i, pl.ds(8, HALF), :] = jnp.where(first_half, top, pltpu.roll(bottom, HALF, 1))
-        zbuf[2 * i + 1, pl.ds(8, HALF), :] = jnp.where(first_half, pltpu.roll(top, HALF, 1), bottom)
-        return carry
-
-    lax.fori_loop(0, COMPS // 2, turn_to_z, 0)
-    send(4, zbuf.at[:, pl.ds(8, 8), :], zhi, "zlo")
-    send(5, zbuf.at[:, pl.ds(HALF, 8), :], zlo, "zhi")
+    def send_row(r, slot):
+        to = ranked(r)
+        pltpu.make_async_remote_copy(
+            src_ref=contrib.at[to],
+            dst_ref=rows1.at[slot],
+            send_sem=s1_send,
+            recv_sem=s1_recv,
+            device_id={"gx": to},
+            device_id_type=MESH,
+        ).start()
+        return 0
 
     loads[2].wait()
 
@@ -335,7 +329,11 @@
 
         def line(k, sign):
             near = [
-                jnp.where(low, ybuf[k, pl.ds(8 * j, 8), :], ybuf[k, pl.ds(ROWS - 8 - 8 * j, 8), :])
+                jnp.where(
+                    low,
+                    rec[k, pl.ds(j, CX, stride=CY), :],
+                    rec[k, pl.ds(CY - 1 - j, CX, stride=CY), :],
+                )
                 for j in range(3)
             ]
             ghost = [sign * x for x in near]
@@ -360,19 +358,36 @@
         contrib[...] = total.reshape(nx, 1, LANES)
         rows1[0] = contrib[gx]
 
-        def send_row(j, carry):
-            to = lax.rem(gx + j, nx)
-            pltpu.make_async_remote_copy(
-                src_ref=contrib.at[to],
-                dst_ref=rows1.at[j],
-                send_sem=s1_send,
-                recv_sem=s1_recv,
-                device_id={"gx": to},
-                device_id_type=MESH,
-            ).start()
-            return carry
-
-        lax.fori_loop(1, nx, send_row, 0)
+        lax.fori_loop(0, rank, lambda r, carry: send_row(r, r - rank + nx), 0)
+
+        def signal_row(r, carry):
+            pl.semaphore_signal(ready, inc=1, device_id={"gx": ranked(r)}, device_id_type=MESH)
+            return carry
+
+        lax.fori_loop(0, rank, signal_row, 0)
+
+    def turn_to_y(k, carry):
+        for y in range(CY):
+            ybuf[k, pl.ds(8 * y, 8), :] = rec[k, pl.ds(y, CX, stride=CY), :]
+        return carry
+
+    lax.fori_loop(0, COMPS, turn_to_y, 0)
+    send(2, ybuf.at[:, pl.ds(0, 24), :], yhi, "ylo")
+    send(3, ybuf.at[:, pl.ds(ROWS - 24, 24), :], ylo, "yhi")
+
+    first_half = iota((HALF, LANES), 1) < HALF
+
+    def turn_to_z(i, carry):
+        both = rec[pl.ds(2 * i, 2), :, :].reshape(2 * ROWS, CZ).T
+        top = both[:HALF]
+        bottom = both[HALF:]
+        zbuf[2 * i, pl.ds(8, HALF), :] = jnp.where(first_half, top, pltpu.roll(bottom, HALF, 1))
+        zbuf[2 * i + 1, pl.ds(8, HALF), :] = jnp.where(first_half, pltpu.roll(top, HALF, 1), bottom)
+        return carry
+
+    lax.fori_loop(0, COMPS // 2, turn_to_z, 0)
+    send(4, zbuf.at[:, pl.ds(8, 8), :], zhi, "zlo")
+    send(5, zbuf.at[:, pl.ds(HALF, 8), :], zlo, "zhi")
 
     loads[1].wait()
     hot = react[...] > 0
@@ -384,13 +399,13 @@
     start = jnp.dot(above, sums.astype(BF16), preferred_element_type=F32)
     slot = iota((ROWS, CAP), 1).astype(F32)
     row_hot = one_where((start <= slot) & (slot < start + sums))
-    rank = jnp.where(hot, start[:, :CZ] + within, 0.0).astype(BF16)
+    order = jnp.where(hot, start[:, :CZ] + within, 0.0).astype(BF16)
     sums_t = dot_nt(jnp.ones((CAP, CZ), BF16), flags)
     before = one_where(iota((ROWS, ROWS), 0) < iota((ROWS, ROWS), 1)).astype(BF16)
     start_t = jnp.dot(sums_t.astype(BF16), before, preferred_element_type=F32)
     slot_t = iota((CAP, ROWS), 0).astype(F32)
     row_hot_t = one_where((start_t <= slot_t) & (slot_t < start_t + sums_t)).astype(BF16)
-    line_rank = jnp.dot(row_hot_t, rank, preferred_element_type=F32)
+    line_rank = jnp.dot(row_hot_t, order, preferred_element_type=F32)
     lane_hot = one_where(line_rank == iota((CAP, CZ), 0).astype(F32) + 1.0).astype(BF16)
 
     cells = rec[...].reshape(COMPS * ROWS, CZ).astype(BF16)
@@ -410,10 +425,112 @@
         COMPS, ROWS, CZ
     )
 
+    def faces(load, normal, flux):
+        def weno_step(k, carry):
+            left, right = weno_pair(load(k))
+            st_l[k] = left
+            st_r[k] = right
+            return carry
+
+        lax.fori_loop(0, COMPS, weno_step, 0)
+
+        def flux_step(i, carry):
+            span = pl.ds(i * 3, 3)
+            left = [st_l[k, span] for k in range(COMPS)]
+            right = [st_r[k, span] for k in range(COMPS)]
+            for k, x in enumerate(hllc(left, right, normal)):
+                flux[k, span] = x
+            return carry
+
+        lax.fori_loop(0, 3, flux_step, 0)
+
+    def sign_of(k, normal):
+        return jnp.where(k == 1 + normal, -1.0, 1.0).astype(F32)
+
+    sends[4].wait_recv()
+    sends[5].wait_recv()
+    first_lanes = iota((8, LANES), 1) < HALF
+
+    def ghosts_z(k, carry):
+        zbuf[k, pl.ds(0, 8), :] = pltpu.roll(
+            jnp.where(first_lanes, zbuf[k, pl.ds(HALF, 8), :], zlo[k]), HALF, 1
+        )
+        zbuf[k, pl.ds(HALF + 8, 8), :] = pltpu.roll(
+            jnp.where(first_lanes, zhi[k], zbuf[k, pl.ds(8, 8), :]), HALF, 1
+        )
+        return carry
+
+    lax.fori_loop(0, COMPS, ghosts_z, 0)
+    lane_low = iota((1, LANES), 1) < HALF
+
+    @pl.when(gz == 0)
+    def _():
+        def mirror(k, carry):
+            for j in range(3):
+                here = zbuf[k, pl.ds(7 - j, 1), :]
+                inside = zbuf[k, pl.ds(8 + j, 1), :] * sign_of(k, 2)
+                zbuf[k, pl.ds(7 - j, 1), :] = jnp.where(lane_low, inside, here)
+            return carry
+
+        lax.fori_loop(0, COMPS, mirror, 0)
+
+    @pl.when(gz == nz - 1)
+    def _():
+        def mirror(k, carry):
+            for j in range(3):
+                here = zbuf[k, pl.ds(HALF + 8 + j, 1), :]
+                inside = zbuf[k, pl.ds(HALF + 7 - j, 1), :] * sign_of(k, 2)
+                zbuf[k, pl.ds(HALF + 8 + j, 1), :] = jnp.where(lane_low, here, inside)
+            return carry
+
+        lax.fori_loop(0, COMPS, mirror, 0)
+
+    faces(
+        lambda k: jnp.stack([zbuf[k, pl.ds(5 + j, 8, stride=8), :] for j in range(14)]), 2, flux_z
+    )
+
+    def mirror_planes(inner, low, high, normal, place, count):
+        @pl.when(place == 0)
+        def _():
+            def mirror(k, carry):
+                for j in range(3):
+                    low[k, pl.ds(16 - 8 * j, 8), :] = inner[k, pl.ds(8 * j, 8), :] * sign_of(k, normal)
+                return carry
+
+            lax.fori_loop(0, COMPS, mirror, 0)
+
+        @pl.when(place == count - 1)
+        def _():
+            def mirror(k, carry):
+                for j in range(3):
+                    high[k, pl.ds(8 * j, 8), :] = inner[k, pl.ds(ROWS - 8 - 8 * j, 8), :] * sign_of(
+                        k, normal
+                    )
+                return carry
+
+            lax.fori_loop(0, COMPS, mirror, 0)
+
+    def planes(low, inner, high):
+        def load(k):
+            return jnp.concatenate(
+                [low[k].reshape(3, 8, CZ), inner[k].reshape(8, 8, CZ), high[k].reshape(3, 8, CZ)]
+            )
+
+        return load
+
+    sends[2].wait_recv()
+    sends[3].wait_recv()
+    mirror_planes(ybuf, ylo, yhi, 1, gy, ny)
+    faces(planes(ylo, ybuf, yhi), 1, flux_y)
     slot_of = (gy // jnp.int32(max(ny - 1, 1))) * nz + gz
 
     @pl.when(is_wall)
     def _():
+        @pl.when(rank < nx - 1)
+        def _():
+            pl.semaphore_wait(ready, nx - 1 - rank)
+            lax.fori_loop(rank + 1, nx, lambda r, carry: send_row(r, r - rank), 0)
+
         pltpu.make_async_copy(rows1.at[pl.ds(1, nx - 1)], rows1.at[pl.ds(1, nx - 1)], s1_recv).wait()
         own[...] = jnp.sum(rows1[...], axis=0)
         parts[slot_of] = own[...]
@@ -432,103 +549,6 @@
 
         lax.fori_loop(1, group, send_part, 0)
 
-    def faces(load, normal, flux):
-        def weno_step(k, carry):
-            left, right = weno_pair(load(k))
-            st_l[k] = left
-            st_r[k] = right
-            return carry
-
-        lax.fori_loop(0, COMPS, weno_step, 0)
-
-        def flux_step(i, carry):
-            span = pl.ds(i * 3, 3)
-            left = [st_l[k, span] for k in range(COMPS)]
-            right = [st_r[k, span] for k in range(COMPS)]
-            for k, x in enumerate(hllc(left, right, normal)):
-                flux[k, span] = x
-            return carry
-
-        lax.fori_loop(0, 3, flux_step, 0)
-
-    def sign_of(k, normal):
-        return jnp.where(k == 1 + normal, -1.0, 1.0).astype(F32)
-
-    sends[4].wait_recv()
-    sends[5].wait_recv()
-    first_lanes = iota((8, LANES), 1) < HALF
-
-    def ghosts_z(k, carry):
-        zbuf[k, pl.ds(0, 8), :] = pltpu.roll(
-            jnp.where(first_lanes, zbuf[k, pl.ds(HALF, 8), :], zlo[k]), HALF, 1
-        )
-        zbuf[k, pl.ds(HALF + 8, 8), :] = pltpu.roll(
-            jnp.where(first_lanes, zhi[k], zbuf[k, pl.ds(8, 8), :]), HALF, 1
-        )
-        return carry
-
-    lax.fori_loop(0, COMPS, ghosts_z, 0)
-    lane_low = iota((1, LANES), 1) < HALF
-
-    @pl.when(gz == 0)
-    def _():
-        def mirror(k, carry):
-            for j in range(3):
-                here = zbuf[k, pl.ds(7 - j, 1), :]
-                inside = zbuf[k, pl.ds(8 + j, 1), :] * sign_of(k, 2)
-                zbuf[k, pl.ds(7 - j, 1), :] = jnp.where(lane_low, inside, here)
-            return carry
-
-        lax.fori_loop(0, COMPS, mirror, 0)
-
-    @pl.when(gz == nz - 1)
-    def _():
-        def mirror(k, carry):
-            for j in range(3):
-                here = zbuf[k, pl.ds(HALF + 8 + j, 1), :]
-                inside = zbuf[k, pl.ds(HALF + 7 - j, 1), :] * sign_of(k, 2)
-                zbuf[k, pl.ds(HALF + 8 + j, 1), :] = jnp.where(lane_low, here, inside)
-            return carry
-
-        lax.fori_loop(0, COMPS, mirror, 0)
-
-    faces(
-        lambda k: jnp.stack([zbuf[k, pl.ds(5 + j, 8, stride=8), :] for j in range(14)]), 2, flux_z
-    )
-
-    def mirror_planes(inner, low, high, normal, place, count):
-        @pl.when(place == 0)
-        def _():
-            def mirror(k, carry):
-                for j in range(3):
-                    low[k, pl.ds(16 - 8 * j, 8), :] = inner[k, pl.ds(8 * j, 8), :] * sign_of(k, normal)
-                return carry
-
-            lax.fori_loop(0, COMPS, mirror, 0)
-
-        @pl.when(place == count - 1)
-        def _():
-            def mirror(k, carry):
-                for j in range(3):
-                    high[k, pl.ds(8 * j, 8), :] = inner[k, pl.ds(ROWS - 8 - 8 * j, 8), :] * sign_of(
-                        k, normal
-                    )
-                return carry
-
-            lax.fori_loop(0, COMPS, mirror, 0)
-
-    def planes(low, inner, high):
-        def load(k):
-            return jnp.concatenate(
-                [low[k].reshape(3, 8, CZ), inner[k].reshape(8, 8, CZ), high[k].reshape(3, 8, CZ)]
-            )
-
-        return load
-
-    sends[2].wait_recv()
-    sends[3].wait_recv()
-    mirror_planes(ybuf, ylo, yhi, 1, gy, ny)
-    faces(planes(ylo, ybuf, yhi), 1, flux_y)
     sends[0].wait_recv()
     sends[1].wait_recv()
     mirror_planes(rec, xlo, xhi, 0, gx, nx)
@@ -585,17 +605,18 @@
 def body(fields, reacting, panel_map, layer_one, layer_two, layer_three, layer_four):
     sizes = (lax.axis_size("gx"), lax.axis_size("gy"), lax.axis_size("gz"))
     nx, ny, nz = sizes
-    any_spec = pl.BlockSpec(memory_space=pl.ANY)
+    any_spec = pl.BlockSpec(memory_space=pltpu.HBM)
     vmem_spec = pl.BlockSpec(memory_space=pltpu.VMEM)
     plane = (COMPS, ROWS, CZ)
     ghost = (COMPS, 24, CZ)
     state = (COMPS, 9, 8, CZ)
     dma = pltpu.SemaphoreType.DMA
+    held = pltpu.with_memory_space_constraint
     new_fields, impulse = pl.pallas_call(
         functools.partial(kernel, sizes),
         out_shape=(
-            jax.ShapeDtypeStruct(plane, F32),
-            jax.ShapeDtypeStruct((8, LANES), F32),
+            pltpu.VMEM(plane, F32),
+            pltpu.VMEM((8, LANES), F32),
         ),
         in_specs=[any_spec] * 7,
         out_specs=(vmem_spec, vmem_spec),
@@ -637,18 +658,19 @@
             dma(()),
             dma(()),
             dma(()),
+            pltpu.SemaphoreType.REGULAR,
         ],
         compiler_params=pltpu.CompilerParams(
             collective_id=0, has_side_effects=True, vmem_limit_bytes=48 * 2**20
         ),
     )(
-        fields.reshape(plane),
-        reacting.reshape(ROWS, CZ),
-        panel_map,
-        layer_one.T,
-        layer_two,
-        layer_three,
-        layer_four,
+        held(fields.reshape(plane), pltpu.HBM),
+        held(reacting.reshape(ROWS, CZ), pltpu.HBM),
+        held(panel_map, pltpu.HBM),
+        held(layer_one.T, pltpu.HBM),
+        held(layer_two, pltpu.HBM),
+        held(layer_three, pltpu.HBM),
+        held(layer_four, pltpu.HBM),
     )
     own_panels = 2 * nx * nz * (CZ // PATCH) // (nx * ny * nz)
     return new_fields.reshape(fields.shape), impulse[0, :own_panels]

time: 41.8 us -> 31.3 us (0.75)
  local copies, waits for them, and re-layouts: 8.09 us -> 1.26 us
  Pallas kernels: 32.4 us -> 29.1 us
    unnamed x15 -> x1, local copies, waits for them, and re-layouts: 7.57 us -> 0.75 us
    pallas_call x1, Pallas kernels: 32.4 us -> 29.1 us  [body(): pl.pallas_call(functools.partial(kernel, sizes), out_shape=(pltpu.VMEM(pl...]
where the time goes in v2:
time: 31.3 us; the launch traced here: 31 us
  Pallas kernels  29.1 us (93%)
  local copies, waits for them, and re-layouts  1.26 us (4%)
  between operations  0.64 us (2%)
    pallas_call x1, Pallas kernels, body(): pl.pallas_call(functools.partial(kernel, sizes), out_shape=(pltpu.VMEM(pl...  29.1 us
    unnamed x1, local copies, waits for them, and re-layouts  0.75 us

profile of v2, /device:TPU:1, one launch (start us, length us, event | category | flops | bytes accessed | tf_op | source)
XLA Modules:
  0.0 31.0 jit_solution(12176308926591064111)
XLA Ops:
  0.6 29.1 %shard_map.86 = (f32[12,64,128]{2,1,0:T(8,128)S(1)}, f32[8,128]{1,0:T(8,128)S(1)}) custom-call(f32[12,64,128]{2,1,0:T(8,128)} %bitcast.7, s32[64,128]{1,0:T(8,128)} %bitcast.9, s32[2,8,128]{2,1,0:T(8,128)} %pmap_hbm.1, bf16[12,1600]{1,0:T(8,128)(2,1)} %bitcast.8, bf16[800,1600]{1,0:T(8,128)(2,1)} %w2_hbm.1, bf16[400,800]{1,0:T(8,128)(2,1)} %w3_hbm.1, ...), custom_call_target="tpu_custom_call" | custom-call | tf_op jit(solution)/shard_map/pallas_call | solution.py:615
  29.8 0.7 %copy.10 = f32[12,8,8,128]{3,2,1,0:T(8,128)} copy(f32[12,8,8,128]{3,2,1,0:T(8,128)S(1)} %bitcast.6) | data formatting | bytes 786432
  30.5 0.5 %slice_bitcast_fusion = f32[8]{0:T(128)} fusion(f32[8,128]{1,0:T(8,128)S(1)} %get-tuple-element.5), kind=kLoop, calls=%fused_computation | loop fusion | bytes 64 | tf_op jit(solution)/shard_map/squeeze | solution.py:676

commit v3 on v2

--- a/solution.py
+++ b/solution.py
@@ -36,6 +36,14 @@
 def recip(x):
     r = pl.reciprocal(x, approx=True)
     return r * (2.0 - x * r)
+
+
+def primitive(rho, momentum, energy):
+    inv = recip(rho)
+    inv = inv * (2.0 - rho * inv)
+    vel = [x * inv for x in momentum]
+    speed = vel[0] * vel[0] + vel[1] * vel[1] + vel[2] * vel[2]
+    return jnp.log(rho), vel, jnp.log(0.4 * (energy - 0.5 * rho * speed)), inv
 
 
 def weno_pair(v):
@@ -187,7 +195,7 @@
     hid2,
     source,
     contrib,
-    rows1,
+    rows2,
     parts,
     own,
     load_sem,
@@ -198,6 +206,7 @@
     s2_send,
     s2_recv,
     ready,
+    late,
 ):
     nx, ny, nz = sizes
     gx = lax.axis_index("gx")
@@ -207,6 +216,7 @@
     group = ny * nz
     me = gy * nz + gz
     walls = 2 * nz
+    mine = 2 * nx * nz * (CZ // PATCH) // (nx * ny * nz)
 
     loads = []
     for i, (src, dst) in enumerate(
@@ -233,64 +243,178 @@
         "zlo": {"gz": lax.rem(gz + nz - 1, nz)},
         "zhi": {"gz": lax.rem(gz + 1, nz)},
     }
-    for where in around.values():
-        pl.semaphore_signal(barrier, inc=1, device_id=where, device_id_type=MESH)
+    half = nx // 2
+    rank = lax.rem(gx, half)
+    side = gx // half
+    has_low = gx > 0
+    has_high = gx < nx - 1
+    late_low = gx == half
+    late_high = gx == half - 1
+
+    def greet(where):
+        pl.semaphore_signal(barrier, inc=1, device_id=around[where], device_id_type=MESH)
+
+    for where in ("ylo", "yhi", "zlo", "zhi"):
+        greet(where)
+
+    @pl.when(has_low)
+    def _():
+        greet("xlo")
+
+    @pl.when(has_high & jnp.logical_not(late_high))
+    def _():
+        greet("xhi")
 
     def greet_wall(w, carry):
-        to_y = (w // nz) * (ny - 1)
+        to_side = w // walls
+        to_y = lax.rem(w // nz, 2) * (ny - 1)
         to_z = lax.rem(w, nz)
 
-        @pl.when(to_y * nz + to_z != me)
+        @pl.when((to_side != side) | (to_y * nz + to_z != me))
         def _():
             pl.semaphore_signal(
-                barrier, inc=1, device_id={"gy": to_y, "gz": to_z}, device_id_type=MESH
+                barrier,
+                inc=1,
+                device_id={"gx": to_side * half + rank, "gy": to_y, "gz": to_z},
+                device_id_type=MESH,
             )
 
         return carry
 
-    lax.fori_loop(0, walls, greet_wall, 0)
-
-    half = nx // 2
-    rank = lax.rem(gx, half) * 2 + gx // half
+    lax.fori_loop(0, 2 * walls, greet_wall, 0)
 
     def ranked(r):
-        return lax.rem(r, 2) * half + r // 2
+        return side * half + r
+
+    def greet_row(r, carry):
+        pl.semaphore_signal(barrier, inc=1, device_id={"gx": ranked(r)}, device_id_type=MESH)
+        return carry
+
+    lax.fori_loop(rank + 1, half, greet_row, 0)
+
+    slot_of = side * walls + (gy // jnp.int32(max(ny - 1, 1))) * nz + gz
+    loads[0].wait()
+
+    def send_row(r, slot):
+        pltpu.make_async_remote_copy(
+            src_ref=own,
+            dst_ref=rows2.at[slot],
+            send_sem=s2_send,
+            recv_sem=s2_recv,
+            device_id={"gx": ranked(r)},
+            device_id_type=MESH,
+        ).start()
+        return 0
+
+    loads[2].wait()
 
     @pl.when(is_wall)
     def _():
-        def greet_row(r, carry):
-            pl.semaphore_signal(barrier, inc=1, device_id={"gx": ranked(r)}, device_id_type=MESH)
-            return carry
-
-        lax.fori_loop(rank + 1, nx, greet_row, 0)
-
-    loads[0].wait()
+        low = gy == 0
+
+        near_of = {0: [], 2: [], 4: []}
+        for j in range(3):
+            rho, *momentum, energy = (
+                jnp.where(
+                    low,
+                    fields[k, pl.ds(j, CX, stride=CY), :],
+                    fields[k, pl.ds(CY - 1 - j, CX, stride=CY), :],
+                )
+                for k in range(5)
+            )
+            log_rho, vel, log_pressure, _ = primitive(rho, momentum, energy)
+            near_of[0].append(log_rho)
+            near_of[2].append(vel[1])
+            near_of[4].append(log_pressure)
+
+        def line(k, sign):
+            near = near_of[k]
+            ghost = [sign * x for x in near]
+            below = ghost[::-1] + near
+            above = near[::-1] + ghost
+            return jnp.stack([jnp.where(low, i, j) for i, j in zip(below, above)])
+
+        left, right = {}, {}
+        for k in (0, 2, 4):
+            left[k], right[k] = weno_pair(line(k, -1.0 if k == 2 else 1.0))
+        push = hllc(left, right, 1, only_push=True)[0] * (1.0 / (PATCH * PATCH))
+        ids = jnp.where(low, pmap[0], pmap[1])
+        total = jnp.zeros((2 * group, LANES), F32)
+        for h in range(2):
+            value = jnp.sum(push[4 * h : 4 * h + 4], axis=0, keepdims=True)
+            panel = ids[4 * h : 4 * h + 1]
+            owner = panel // mine
+            owner_x = owner // group
+            member = owner_x // half * group + owner % group
+            place = owner_x % half * mine + panel % mine
+            spread = jnp.where(iota((2 * group, LANES), 0) == member, value, 0.0)
+            lane = one_where(iota((LANES, LANES), 0) == place).astype(BF16)
+            big = spread.astype(BF16)
+            small = (spread - big.astype(F32)).astype(BF16)
+            total = total + dot_nt(big, lane) + dot_nt(small, lane)
+        contrib[...] = total.reshape(2 * group, 1, LANES)
+        parts[slot_of] = contrib[side * group + me]
 
     def recon_step(i, carry):
         span = pl.ds(pl.multiple_of(i * 16, 16), 16)
-        rho = fields[0, span, :]
-        inv = recip(rho)
-        inv = inv * (2.0 - rho * inv)
-        vel = [fields[k, span, :] * inv for k in (1, 2, 3)]
-        speed = vel[0] * vel[0] + vel[1] * vel[1] + vel[2] * vel[2]
-        pressure = 0.4 * (fields[4, span, :] - 0.5 * rho * speed)
-        rec[0, span, :] = jnp.log(rho)
+        rho, *momentum, energy = (fields[k, span, :] for k in range(5))
+        log_rho, vel, log_pressure, inv = primitive(rho, momentum, energy)
+        rec[0, span, :] = log_rho
         for k in range(3):
             rec[1 + k, span, :] = vel[k]
-        rec[4, span, :] = jnp.log(pressure)
+        rec[4, span, :] = log_pressure
         for k in range(5, COMPS):
             rec[k, span, :] = fields[k, span, :] * inv
         return carry
 
-    lax.fori_loop(0, ROWS // 16, recon_step, 0)
+    waits_long = rank >= half - half // 4
+
+    @pl.when(waits_long)
+    def _():
+        lax.fori_loop(0, ROWS // 16, recon_step, 0)
+
+    linked = (
+        4
+        + has_high.astype(jnp.int32)
+        + (has_low & jnp.logical_not(late_low)).astype(jnp.int32)
+        + rank
+        + is_wall.astype(jnp.int32) * (2 * group - 1)
+    )
+    pl.semaphore_wait(barrier, linked)
+
+    @pl.when(late_high)
+    def _():
+        pl.semaphore_signal(late, inc=1, device_id=around["xhi"], device_id_type=MESH)
 
     @pl.when(is_wall)
     def _():
-        pl.semaphore_wait(barrier, 6 + rank + group - 1)
-
-    @pl.when(jnp.logical_not(is_wall))
-    def _():
-        pl.semaphore_wait(barrier, 6)
+        def send_part(j, carry):
+            to = lax.rem(side * group + me + j, 2 * group)
+            pltpu.make_async_remote_copy(
+                src_ref=contrib.at[to],
+                dst_ref=parts.at[slot_of],
+                send_sem=s1_send,
+                recv_sem=s1_recv,
+                device_id={
+                    "gx": to // group * half + rank,
+                    "gy": lax.rem(to // nz, ny),
+                    "gz": lax.rem(to, nz),
+                },
+                device_id_type=MESH,
+            ).start()
+            return carry
+
+        lax.fori_loop(1, 2 * group, send_part, 0)
+
+    def signal_row(r, carry):
+        pl.semaphore_signal(ready, inc=1, device_id={"gx": ranked(r)}, device_id_type=MESH)
+        return carry
+
+    lax.fori_loop(0, rank, signal_row, 0)
+
+    @pl.when(jnp.logical_not(waits_long))
+    def _():
+        lax.fori_loop(0, ROWS // 16, recon_step, 0)
 
     sends = []
 
@@ -303,68 +427,20 @@
             device_id=around[where],
             device_id_type=MESH,
         )
-        copy.start()
         sends.append(copy)
-
-    send(0, rec.at[:, pl.ds(0, 24), :], xhi, "xlo")
-    send(1, rec.at[:, pl.ds(ROWS - 24, 24), :], xlo, "xhi")
-
-    def send_row(r, slot):
-        to = ranked(r)
-        pltpu.make_async_remote_copy(
-            src_ref=contrib.at[to],
-            dst_ref=rows1.at[slot],
-            send_sem=s1_send,
-            recv_sem=s1_recv,
-            device_id={"gx": to},
-            device_id_type=MESH,
-        ).start()
-        return 0
-
-    loads[2].wait()
-
-    @pl.when(is_wall)
-    def _():
-        low = gy == 0
-
-        def line(k, sign):
-            near = [
-                jnp.where(
-                    low,
-                    rec[k, pl.ds(j, CX, stride=CY), :],
-                    rec[k, pl.ds(CY - 1 - j, CX, stride=CY), :],
-                )
-                for j in range(3)
-            ]
-            ghost = [sign * x for x in near]
-            below = ghost[::-1] + near
-            above = near[::-1] + ghost
-            return jnp.stack([jnp.where(low, i, j) for i, j in zip(below, above)])
-
-        left, right = {}, {}
-        for k in (0, 2, 4):
-            left[k], right[k] = weno_pair(line(k, -1.0 if k == 2 else 1.0))
-        push = hllc(left, right, 1, only_push=True)[0] * (1.0 / (PATCH * PATCH))
-        ids = jnp.where(low, pmap[0], pmap[1])
-        total = jnp.zeros((nx, LANES), F32)
-        for h in range(2):
-            value = jnp.sum(push[4 * h : 4 * h + 4], axis=0, keepdims=True)
-            panel = ids[4 * h : 4 * h + 1]
-            spread = jnp.where(iota((nx, LANES), 0) == panel // LANES, value, 0.0)
-            lane = one_where(iota((LANES, LANES), 0) == panel % LANES).astype(BF16)
-            big = spread.astype(BF16)
-            small = (spread - big.astype(F32)).astype(BF16)
-            total = total + dot_nt(big, lane) + dot_nt(small, lane)
-        contrib[...] = total.reshape(nx, 1, LANES)
-        rows1[0] = contrib[gx]
-
-        lax.fori_loop(0, rank, lambda r, carry: send_row(r, r - rank + nx), 0)
-
-        def signal_row(r, carry):
-            pl.semaphore_signal(ready, inc=1, device_id={"gx": ranked(r)}, device_id_type=MESH)
-            return carry
-
-        lax.fori_loop(0, rank, signal_row, 0)
+        return copy
+
+    to_low = send(0, rec.at[:, pl.ds(0, 24), :], xhi, "xlo")
+    to_high = send(1, rec.at[:, pl.ds(ROWS - 24, 24), :], xlo, "xhi")
+
+    @pl.when(has_low & jnp.logical_not(late_low))
+    def _():
+        to_low.start()
+
+    @pl.when(has_high)
+    def _():
+        to_high.start()
+
 
     def turn_to_y(k, carry):
         for y in range(CY):
@@ -372,8 +448,8 @@
         return carry
 
     lax.fori_loop(0, COMPS, turn_to_y, 0)
-    send(2, ybuf.at[:, pl.ds(0, 24), :], yhi, "ylo")
-    send(3, ybuf.at[:, pl.ds(ROWS - 24, 24), :], ylo, "yhi")
+    send(2, ybuf.at[:, pl.ds(0, 24), :], yhi, "ylo").start()
+    send(3, ybuf.at[:, pl.ds(ROWS - 24, 24), :], ylo, "yhi").start()
 
     first_half = iota((HALF, LANES), 1) < HALF
 
@@ -386,8 +462,8 @@
         return carry
 
     lax.fori_loop(0, COMPS // 2, turn_to_z, 0)
-    send(4, zbuf.at[:, pl.ds(8, 8), :], zhi, "zlo")
-    send(5, zbuf.at[:, pl.ds(HALF, 8), :], zlo, "zhi")
+    send(4, zbuf.at[:, pl.ds(8, 8), :], zhi, "zlo").start()
+    send(5, zbuf.at[:, pl.ds(HALF, 8), :], zlo, "zhi").start()
 
     loads[1].wait()
     hot = react[...] > 0
@@ -408,6 +484,19 @@
     line_rank = jnp.dot(row_hot_t, order, preferred_element_type=F32)
     lane_hot = one_where(line_rank == iota((CAP, CZ), 0).astype(F32) + 1.0).astype(BF16)
 
+    @pl.when(is_wall)
+    def _():
+        few = parts.at[pl.ds(0, 2 * walls - 1)]
+        pltpu.make_async_copy(few, few, s1_recv).wait()
+
+    @pl.when(jnp.logical_not(is_wall))
+    def _():
+        pltpu.make_async_copy(parts, parts, s1_recv).wait()
+
+    own[...] = jnp.sum(parts[...], axis=0)
+    rows2[0] = own[...]
+    lax.fori_loop(0, rank, lambda r, carry: send_row(r, r - rank + half), 0)
+
     cells = rec[...].reshape(COMPS * ROWS, CZ).astype(BF16)
     spread_cells = dot_nt(cells, lane_hot).reshape(COMPS, ROWS, CAP)
     features = jnp.sum(spread_cells * row_hot[None], axis=1).astype(BF16)
@@ -489,6 +578,17 @@
         lambda k: jnp.stack([zbuf[k, pl.ds(5 + j, 8, stride=8), :] for j in range(14)]), 2, flux_z
     )
 
+    def send_up():
+        pl.semaphore_wait(ready, half - 1 - rank)
+        lax.fori_loop(rank + 1, half, lambda r, carry: send_row(r, r - rank), 0)
+
+    goes_up = rank < half - 1
+    goes_early = rank >= half // 2
+
+    @pl.when(goes_up & goes_early)
+    def _():
+        send_up()
+
     def mirror_planes(inner, low, high, normal, place, count):
         @pl.when(place == 0)
         def _():
@@ -522,35 +622,19 @@
     sends[3].wait_recv()
     mirror_planes(ybuf, ylo, yhi, 1, gy, ny)
     faces(planes(ylo, ybuf, yhi), 1, flux_y)
-    slot_of = (gy // jnp.int32(max(ny - 1, 1))) * nz + gz
-
-    @pl.when(is_wall)
-    def _():
-        @pl.when(rank < nx - 1)
-        def _():
-            pl.semaphore_wait(ready, nx - 1 - rank)
-            lax.fori_loop(rank + 1, nx, lambda r, carry: send_row(r, r - rank), 0)
-
-        pltpu.make_async_copy(rows1.at[pl.ds(1, nx - 1)], rows1.at[pl.ds(1, nx - 1)], s1_recv).wait()
-        own[...] = jnp.sum(rows1[...], axis=0)
-        parts[slot_of] = own[...]
-
-        def send_part(j, carry):
-            to = lax.rem(me + j, group)
-            pltpu.make_async_remote_copy(
-                src_ref=own,
-                dst_ref=parts.at[slot_of],
-                send_sem=s2_send,
-                recv_sem=s2_recv,
-                device_id={"gy": to // nz, "gz": lax.rem(to, nz)},
-                device_id_type=MESH,
-            ).start()
-            return carry
-
-        lax.fori_loop(1, group, send_part, 0)
-
-    sends[0].wait_recv()
-    sends[1].wait_recv()
+    @pl.when(late_low)
+    def _():
+        pl.semaphore_wait(late, 1)
+        to_low.start()
+
+    @pl.when(has_high)
+    def _():
+        to_low.wait_recv()
+
+    @pl.when(has_low)
+    def _():
+        to_high.wait_recv()
+
     mirror_planes(rec, xlo, xhi, 0, gx, nx)
     faces(planes(xlo, rec, xhi), 0, flux_x)
 
@@ -577,29 +661,34 @@
 
     lax.fori_loop(0, COMPS // 2, finish, 0)
 
+    @pl.when(goes_up & jnp.logical_not(goes_early))
+    def _():
+        send_up()
+
+    many = pl.ds(1, half - 1)
+    if half > 1:
+        pltpu.make_async_copy(rows2.at[many], rows2.at[many], s2_recv).wait()
+    total = jnp.sum(rows2[...], axis=0)
+    wide = jnp.broadcast_to(total, (8, LANES))
+    imp_ref[...] = pltpu.roll(wide, lax.rem(LANES - rank * mine, LANES), 1)
+    if half > 1:
+        pltpu.make_async_copy(rows2.at[many], rows2.at[many], s2_send).wait()
+
     @pl.when(is_wall)
     def _():
-        few = pl.ds(0, walls - 1)
-        pltpu.make_async_copy(parts.at[few], parts.at[few], s2_recv).wait()
-        many = pl.ds(1, nx - 1)
-        pltpu.make_async_copy(contrib.at[many], contrib.at[many], s1_send).wait()
-
-        def sent(j, carry):
-            pltpu.make_async_copy(own, own, s2_send).wait()
-            return carry
-
-        lax.fori_loop(1, group, sent, 0)
-
-    @pl.when(jnp.logical_not(is_wall))
-    def _():
-        pltpu.make_async_copy(parts, parts, s2_recv).wait()
-
-    total = jnp.sum(parts[...], axis=0)
-    mine = LANES // group
-    wide = jnp.broadcast_to(total, (8, LANES))
-    imp_ref[...] = pltpu.roll(wide, lax.rem(LANES - me * mine, LANES), 1)
-    for copy in sends:
+        most = pl.ds(1, 2 * group - 1)
+        pltpu.make_async_copy(contrib.at[most], contrib.at[most], s1_send).wait()
+
+    for copy in sends[2:]:
         copy.wait_send()
+
+    @pl.when(has_low)
+    def _():
+        to_low.wait_send()
+
+    @pl.when(has_high)
+    def _():
+        to_high.wait_send()
 
 
 def body(fields, reacting, panel_map, layer_one, layer_two, layer_three, layer_four):
@@ -647,9 +736,9 @@
             pltpu.VMEM((H1, CAP), BF16),
             pltpu.VMEM((H2, CAP), BF16),
             pltpu.VMEM(plane, F32),
-            pltpu.VMEM((nx, 1, LANES), F32),
-            pltpu.VMEM((nx, 1, LANES), F32),
-            pltpu.VMEM((2 * nz, 1, LANES), F32),
+            pltpu.VMEM((2 * ny * nz, 1, LANES), F32),
+            pltpu.VMEM((nx // 2, 1, LANES), F32),
+            pltpu.VMEM((4 * nz, 1, LANES), F32),
             pltpu.VMEM((1, LANES), F32),
             dma((7,)),
             dma((6,)),
@@ -658,6 +747,7 @@
             dma(()),
             dma(()),
             dma(()),
+            pltpu.SemaphoreType.REGULAR,
             pltpu.SemaphoreType.REGULAR,
         ],
         compiler_params=pltpu.CompilerParams(

time: 31.3 us -> 28.2 us (0.901)
  Pallas kernels: 29.1 us -> 25.9 us
    pallas_call x1, Pallas kernels: 29.1 us -> 25.9 us  [body(): pl.pallas_call(functools.partial(kernel, sizes), out_shape=(pltpu.VMEM(pl...]
where the time goes in v3:
time: 28.2 us; the launch traced here: 27.8 us
  Pallas kernels  25.9 us (92%)
  local copies, waits for them, and re-layouts  1.26 us (4%)
  between operations  0.64 us (2%)
    pallas_call x1, Pallas kernels, body(): pl.pallas_call(functools.partial(kernel, sizes), out_shape=(pltpu.VMEM(pl...  25.9 us
    unnamed x1, local copies, waits for them, and re-layouts  0.75 us

profile of v3, /device:TPU:1, one launch (start us, length us, event | category | flops | bytes accessed | tf_op | source)
XLA Modules:
  0.0 27.8 jit_solution(11543501433926517355)
XLA Ops:
  0.6 25.9 %shard_map.86 = (f32[12,64,128]{2,1,0:T(8,128)S(1)}, f32[8,128]{1,0:T(8,128)S(1)}) custom-call(f32[12,64,128]{2,1,0:T(8,128)} %bitcast.7, s32[64,128]{1,0:T(8,128)} %bitcast.9, s32[2,8,128]{2,1,0:T(8,128)} %pmap_hbm.1, bf16[12,1600]{1,0:T(8,128)(2,1)} %bitcast.8, bf16[800,1600]{1,0:T(8,128)(2,1)} %w2_hbm.1, bf16[400,800]{1,0:T(8,128)(2,1)} %w3_hbm.1, ...), custom_call_target="tpu_custom_call" | custom-call | tf_op jit(solution)/shard_map/pallas_call | solution.py:704
  26.5 0.7 %copy.10 = f32[12,8,8,128]{3,2,1,0:T(8,128)} copy(f32[12,8,8,128]{3,2,1,0:T(8,128)S(1)} %bitcast.6) | data formatting | bytes 786432
  27.3 0.5 %slice_bitcast_fusion = f32[8]{0:T(128)} fusion(f32[8,128]{1,0:T(8,128)S(1)} %get-tuple-element.5), kind=kLoop, calls=%fused_computation | loop fusion | bytes 64 | tf_op jit(solution)/shard_map/squeeze | solution.py:766

commit v4 on v3

--- a/solution.py
+++ b/solution.py
@@ -231,7 +231,8 @@
         )
     ):
         copy = pltpu.make_async_copy(src, dst, load_sem.at[i])
-        copy.start()
+        if i < 3:
+            copy.start()
         loads.append(copy)
 
     barrier = pltpu.get_barrier_semaphore()
@@ -251,6 +252,31 @@
     late_low = gx == half
     late_high = gx == half - 1
 
+    xs = [side * half + rank, (1 - side) * half + rank]
+    sides = [side, 1 - side]
+    ys = [gy] + [lax.rem(gy + i, ny) for i in range(1, ny)]
+    zs = [gz] + [lax.rem(gz + i, nz) for i in range(1, nz)]
+
+    def far_first(count):
+        return sorted(range(count), key=lambda i: -min(i, count - i))
+
+    for ds in (1, 0):
+        for dz in far_first(nz):
+            for to_y in (0, ny - 1):
+
+                def greet_wall(ds=ds, dz=dz, to_y=to_y):
+                    pl.semaphore_signal(
+                        barrier,
+                        inc=1,
+                        device_id={"gx": xs[ds], "gy": jnp.int32(to_y), "gz": zs[dz]},
+                        device_id_type=MESH,
+                    )
+
+                if ds == 0 and dz == 0:
+                    pl.when(gy != to_y)(greet_wall)
+                else:
+                    greet_wall()
+
     def greet(where):
         pl.semaphore_signal(barrier, inc=1, device_id=around[where], device_id_type=MESH)
 
@@ -264,24 +290,6 @@
     @pl.when(has_high & jnp.logical_not(late_high))
     def _():
         greet("xhi")
-
-    def greet_wall(w, carry):
-        to_side = w // walls
-        to_y = lax.rem(w // nz, 2) * (ny - 1)
-        to_z = lax.rem(w, nz)
-
-        @pl.when((to_side != side) | (to_y * nz + to_z != me))
-        def _():
-            pl.semaphore_signal(
-                barrier,
-                inc=1,
-                device_id={"gx": to_side * half + rank, "gy": to_y, "gz": to_z},
-                device_id_type=MESH,
-            )
-
-        return carry
-
-    lax.fori_loop(0, 2 * walls, greet_wall, 0)
 
     def ranked(r):
         return side * half + r
@@ -381,6 +389,8 @@
         + is_wall.astype(jnp.int32) * (2 * group - 1)
     )
     pl.semaphore_wait(barrier, linked)
+    for copy in loads[3:]:
+        copy.start()
 
     @pl.when(late_high)
     def _():
@@ -388,29 +398,44 @@
 
     @pl.when(is_wall)
     def _():
-        def send_part(j, carry):
-            to = lax.rem(side * group + me + j, 2 * group)
-            pltpu.make_async_remote_copy(
-                src_ref=contrib.at[to],
-                dst_ref=parts.at[slot_of],
-                send_sem=s1_send,
-                recv_sem=s1_recv,
-                device_id={
-                    "gx": to // group * half + rank,
-                    "gy": lax.rem(to // nz, ny),
-                    "gz": lax.rem(to, nz),
-                },
-                device_id_type=MESH,
-            ).start()
-            return carry
-
-        lax.fori_loop(1, 2 * group, send_part, 0)
+        for ds in (1, 0):
+            for dy in far_first(ny):
+                for dz in far_first(nz):
+                    if ds or dy or dz:
+                        pltpu.make_async_remote_copy(
+                            src_ref=contrib.at[sides[ds] * group + ys[dy] * nz + zs[dz]],
+                            dst_ref=parts.at[slot_of],
+                            send_sem=s1_send,
+                            recv_sem=s1_recv,
+                            device_id={"gx": xs[ds], "gy": ys[dy], "gz": zs[dz]},
+                            device_id_type=MESH,
+                        ).start()
 
     def signal_row(r, carry):
         pl.semaphore_signal(ready, inc=1, device_id={"gx": ranked(r)}, device_id_type=MESH)
         return carry
 
     lax.fori_loop(0, rank, signal_row, 0)
+
+    def pass_on():
+        @pl.when(is_wall)
+        def _():
+            few = parts.at[pl.ds(0, 2 * walls - 1)]
+            pltpu.make_async_copy(few, few, s1_recv).wait()
+
+        @pl.when(jnp.logical_not(is_wall))
+        def _():
+            pltpu.make_async_copy(parts, parts, s1_recv).wait()
+
+        own[...] = jnp.sum(parts[...], axis=0)
+        rows2[0] = own[...]
+        lax.fori_loop(0, rank, lambda r, carry: send_row(r, r - rank + half), 0)
+
+    in_last = (rank >= half // 2) & (rank < half - half // 4)
+
+    @pl.when(in_last)
+    def _():
+        pass_on()
 
     @pl.when(jnp.logical_not(waits_long))
     def _():
@@ -484,18 +509,9 @@
     line_rank = jnp.dot(row_hot_t, order, preferred_element_type=F32)
     lane_hot = one_where(line_rank == iota((CAP, CZ), 0).astype(F32) + 1.0).astype(BF16)
 
-    @pl.when(is_wall)
-    def _():
-        few = parts.at[pl.ds(0, 2 * walls - 1)]
-        pltpu.make_async_copy(few, few, s1_recv).wait()
-
-    @pl.when(jnp.logical_not(is_wall))
-    def _():
-        pltpu.make_async_copy(parts, parts, s1_recv).wait()
-
-    own[...] = jnp.sum(parts[...], axis=0)
-    rows2[0] = own[...]
-    lax.fori_loop(0, rank, lambda r, carry: send_row(r, r - rank + half), 0)
+    @pl.when((rank >= half // 4) & jnp.logical_not(in_last))
+    def _():
+        pass_on()
 
     cells = rec[...].reshape(COMPS * ROWS, CZ).astype(BF16)
     spread_cells = dot_nt(cells, lane_hot).reshape(COMPS, ROWS, CAP)
@@ -514,6 +530,10 @@
         COMPS, ROWS, CZ
     )
 
+    @pl.when(rank < half // 4)
+    def _():
+        pass_on()
+
     def faces(load, normal, flux):
         def weno_step(k, carry):
             left, right = weno_pair(load(k))
@@ -626,6 +646,12 @@
     def _():
         pl.semaphore_wait(late, 1)
         to_low.start()
+
+    goes_middle = ((rank >= half // 4) & (rank < half // 2)) | (late_low & jnp.logical_not(goes_early))
+
+    @pl.when(goes_up & goes_middle)
+    def _():
+        send_up()
 
     @pl.when(has_high)
     def _():
@@ -661,7 +687,7 @@
 
     lax.fori_loop(0, COMPS // 2, finish, 0)
 
-    @pl.when(goes_up & jnp.logical_not(goes_early))
+    @pl.when(goes_up & jnp.logical_not(goes_early | goes_middle))
     def _():
         send_up()
 

time: 28.2 us -> 27.5 us (0.975); the launches traced: 27.8 us -> 27.4 us
  Pallas kernels: 25.9 us -> 25.5 us
    pallas_call x1, Pallas kernels: 25.9 us -> 25.5 us  [body(): pl.pallas_call(functools.partial(kernel, sizes), out_shape=(pltpu.VMEM(pl...]
where the time goes in v4:
time: 27.5 us; the launch traced here: 27.4 us
  Pallas kernels  25.5 us (93%)
  local copies, waits for them, and re-layouts  1.26 us (5%)
  between operations  0.64 us (2%)
    pallas_call x1, Pallas kernels, body(): pl.pallas_call(functools.partial(kernel, sizes), out_shape=(pltpu.VMEM(pl...  25.5 us
    unnamed x1, local copies, waits for them, and re-layouts  0.75 us

profile of v4, /device:TPU:1, one launch (start us, length us, event | category | flops | bytes accessed | tf_op | source)
XLA Modules:
  0.0 27.4 jit_solution(8897487154307663231)
XLA Ops:
  0.6 25.5 %shard_map.86 = (f32[12,64,128]{2,1,0:T(8,128)S(1)}, f32[8,128]{1,0:T(8,128)S(1)}) custom-call(f32[12,64,128]{2,1,0:T(8,128)} %bitcast.7, s32[64,128]{1,0:T(8,128)} %bitcast.9, s32[2,8,128]{2,1,0:T(8,128)} %pmap_hbm.1, bf16[12,1600]{1,0:T(8,128)(2,1)} %bitcast.8, bf16[800,1600]{1,0:T(8,128)(2,1)} %w2_hbm.1, bf16[400,800]{1,0:T(8,128)(2,1)} %w3_hbm.1, ...), custom_call_target="tpu_custom_call" | custom-call | tf_op jit(solution)/shard_map/pallas_call | solution.py:730
  26.1 0.7 %copy.10 = f32[12,8,8,128]{3,2,1,0:T(8,128)} copy(f32[12,8,8,128]{3,2,1,0:T(8,128)S(1)} %bitcast.6) | data formatting | bytes 786432
  26.8 0.5 %slice_bitcast_fusion = f32[8]{0:T(128)} fusion(f32[8,128]{1,0:T(8,128)S(1)} %get-tuple-element.5), kind=kLoop, calls=%fused_computation | loop fusion | bytes 64 | tf_op jit(solution)/shard_map/squeeze | solution.py:792

commit v5 on v4

--- a/solution.py
+++ b/solution.py
@@ -197,6 +197,7 @@
     contrib,
     rows2,
     parts,
+    direct,
     own,
     load_sem,
     send_sem,
@@ -207,6 +208,8 @@
     s2_recv,
     ready,
     late,
+    d_send,
+    d_recv,
 ):
     nx, ny, nz = sizes
     gx = lax.axis_index("gx")
@@ -290,6 +293,30 @@
     @pl.when(has_high & jnp.logical_not(late_high))
     def _():
         greet("xhi")
+
+    firsts = half // 8
+    last_at = half // 2
+    lasts = half // 4 if firsts else 0
+    is_first = rank < firsts
+    in_last = (rank >= last_at) & (rank < half - half // 4)
+
+    if firsts:
+
+        @pl.when(is_first)
+        def _():
+            def greet_last(i, carry):
+                to_x = (i % 2) * half + last_at + i // 4
+                to_y = (i // 2 % 2) * (ny - 1)
+                for to_z in range(nz):
+                    pl.semaphore_signal(
+                        barrier,
+                        inc=1,
+                        device_id={"gx": to_x, "gy": to_y, "gz": jnp.int32(to_z)},
+                        device_id_type=MESH,
+                    )
+                return carry
+
+            lax.fori_loop(0, lasts * 4, greet_last, 0)
 
     def ranked(r):
         return side * half + r
@@ -387,6 +414,7 @@
         + (has_low & jnp.logical_not(late_low)).astype(jnp.int32)
         + rank
         + is_wall.astype(jnp.int32) * (2 * group - 1)
+        + (is_wall & in_last).astype(jnp.int32) * (firsts * 2 * group)
     )
     pl.semaphore_wait(barrier, linked)
     for copy in loads[3:]:
@@ -411,6 +439,30 @@
                             device_id_type=MESH,
                         ).start()
 
+    if firsts:
+
+        @pl.when(is_wall & in_last)
+        def _():
+            def send_direct(i, carry):
+                to_side = i // ny % 2
+                to_y = i % ny
+                for to_z in range(nz):
+                    pltpu.make_async_remote_copy(
+                        src_ref=contrib.at[to_side * group + to_y * nz + to_z],
+                        dst_ref=direct.at[(rank - last_at) * 2 * walls + slot_of],
+                        send_sem=d_send,
+                        recv_sem=d_recv,
+                        device_id={
+                            "gx": to_side * half + i // (2 * ny),
+                            "gy": to_y,
+                            "gz": jnp.int32(to_z),
+                        },
+                        device_id_type=MESH,
+                    ).start()
+                return carry
+
+            lax.fori_loop(0, firsts * 2 * ny, send_direct, 0)
+
     def signal_row(r, carry):
         pl.semaphore_signal(ready, inc=1, device_id={"gx": ranked(r)}, device_id_type=MESH)
         return carry
@@ -429,9 +481,8 @@
 
         own[...] = jnp.sum(parts[...], axis=0)
         rows2[0] = own[...]
-        lax.fori_loop(0, rank, lambda r, carry: send_row(r, r - rank + half), 0)
-
-    in_last = (rank >= half // 2) & (rank < half - half // 4)
+        first = jnp.where(in_last, firsts, 0)
+        lax.fori_loop(first, rank, lambda r, carry: send_row(r, r - rank + half), 0)
 
     @pl.when(in_last)
     def _():
@@ -692,12 +743,48 @@
         send_up()
 
     many = pl.ds(1, half - 1)
-    if half > 1:
+    if firsts:
+
+        @pl.when(is_first)
+        def _():
+            for i in range(lasts):
+                rows2[rank + half - last_at - i] = jnp.zeros((1, LANES), F32)
+            some = pl.ds(1, half - 1 - lasts)
+            pltpu.make_async_copy(rows2.at[some], rows2.at[some], s2_recv).wait()
+            pltpu.make_async_copy(direct, direct, d_recv).wait()
+            rows2[0] += jnp.sum(direct[...], axis=0)
+
+        @pl.when(jnp.logical_not(is_first))
+        def _():
+            pltpu.make_async_copy(rows2.at[many], rows2.at[many], s2_recv).wait()
+
+    elif half > 1:
         pltpu.make_async_copy(rows2.at[many], rows2.at[many], s2_recv).wait()
     total = jnp.sum(rows2[...], axis=0)
     wide = jnp.broadcast_to(total, (8, LANES))
     imp_ref[...] = pltpu.roll(wide, lax.rem(LANES - rank * mine, LANES), 1)
-    if half > 1:
+    if firsts:
+
+        @pl.when(in_last)
+        def _():
+            some = pl.ds(1, half - 1 - firsts)
+            pltpu.make_async_copy(rows2.at[some], rows2.at[some], s2_send).wait()
+
+        @pl.when(jnp.logical_not(in_last))
+        def _():
+            pltpu.make_async_copy(rows2.at[many], rows2.at[many], s2_send).wait()
+
+        @pl.when(is_wall & in_last)
+        def _():
+            every = pl.ds(0, 2 * group)
+
+            def sent(i, carry):
+                pltpu.make_async_copy(contrib.at[every], contrib.at[every], d_send).wait()
+                return carry
+
+            lax.fori_loop(0, firsts, sent, 0)
+
+    elif half > 1:
         pltpu.make_async_copy(rows2.at[many], rows2.at[many], s2_send).wait()
 
     @pl.when(is_wall)
@@ -765,6 +852,7 @@
             pltpu.VMEM((2 * ny * nz, 1, LANES), F32),
             pltpu.VMEM((nx // 2, 1, LANES), F32),
             pltpu.VMEM((4 * nz, 1, LANES), F32),
+            pltpu.VMEM((max(nx // 8, 1) * 4 * nz, 1, LANES), F32),
             pltpu.VMEM((1, LANES), F32),
             dma((7,)),
             dma((6,)),
@@ -775,6 +863,8 @@
             dma(()),
             pltpu.SemaphoreType.REGULAR,
             pltpu.SemaphoreType.REGULAR,
+            dma(()),
+            dma(()),
         ],
         compiler_params=pltpu.CompilerParams(
             collective_id=0, has_side_effects=True, vmem_limit_bytes=48 * 2**20

time: 27.5 us -> 27.1 us (0.985); the launches traced: 27.4 us -> 26.6 us
  Pallas kernels: 25.5 us -> 24.7 us
    pallas_call x1, Pallas kernels: 25.5 us -> 24.7 us  [body(): pl.pallas_call(functools.partial(kernel, sizes), out_shape=(pltpu.VMEM(pl...]
where the time goes in v5:
time: 27.1 us; the launch traced here: 26.6 us
  Pallas kernels  24.7 us (91%)
  local copies, waits for them, and re-layouts  1.26 us (5%)
  between operations  0.64 us (2%)
    pallas_call x1, Pallas kernels, body(): pl.pallas_call(functools.partial(kernel, sizes), out_shape=(pltpu.VMEM(pl...  24.7 us
    unnamed x1, local copies, waits for them, and re-layouts  0.75 us

profile of v5, /device:TPU:1, one launch (start us, length us, event | category | flops | bytes accessed | tf_op | source)
XLA Modules:
  0.0 26.6 jit_solution(10592097081899386986)
XLA Ops:
  0.6 24.7 %shard_map.86 = (f32[12,64,128]{2,1,0:T(8,128)S(1)}, f32[8,128]{1,0:T(8,128)S(1)}) custom-call(f32[12,64,128]{2,1,0:T(8,128)} %bitcast.7, s32[64,128]{1,0:T(8,128)} %bitcast.9, s32[2,8,128]{2,1,0:T(8,128)} %pmap_hbm.1, bf16[12,1600]{1,0:T(8,128)(2,1)} %bitcast.8, bf16[800,1600]{1,0:T(8,128)(2,1)} %w2_hbm.1, bf16[400,800]{1,0:T(8,128)(2,1)} %w3_hbm.1, ...), custom_call_target="tpu_custom_call" | custom-call | tf_op jit(solution)/shard_map/pallas_call | solution.py:817
  25.4 0.7 %copy.10 = f32[12,8,8,128]{3,2,1,0:T(8,128)} copy(f32[12,8,8,128]{3,2,1,0:T(8,128)S(1)} %bitcast.6) | data formatting | bytes 786432
  26.1 0.5 %slice_bitcast_fusion = f32[8]{0:T(128)} fusion(f32[8,128]{1,0:T(8,128)S(1)} %get-tuple-element.5), kind=kLoop, calls=%fused_computation | loop fusion | bytes 64 | tf_op jit(solution)/shard_map/squeeze | solution.py:882

commit v6 on v5

--- a/solution.py
+++ b/solution.py
@@ -408,6 +408,32 @@
     def _():
         lax.fori_loop(0, ROWS // 16, recon_step, 0)
 
+    sends = []
+
+    def send(i, src, dst, where):
+        copy = pltpu.make_async_remote_copy(
+            src_ref=src,
+            dst_ref=dst,
+            send_sem=send_sem.at[i],
+            recv_sem=recv_sem.at[i],
+            device_id=around[where],
+            device_id_type=MESH,
+        )
+        sends.append(copy)
+        return copy
+
+    to_low = send(0, rec.at[:, pl.ds(0, 24), :], xhi, "xlo")
+    to_high = send(1, rec.at[:, pl.ds(ROWS - 24, 24), :], xlo, "xhi")
+
+    def send_x():
+        @pl.when(has_high)
+        def _():
+            to_high.start()
+
+        @pl.when(has_low & jnp.logical_not(late_low))
+        def _():
+            to_low.start()
+
     linked = (
         4
         + has_high.astype(jnp.int32)
@@ -417,6 +443,11 @@
         + (is_wall & in_last).astype(jnp.int32) * (firsts * 2 * group)
     )
     pl.semaphore_wait(barrier, linked)
+
+    @pl.when(waits_long)
+    def _():
+        send_x()
+
     for copy in loads[3:]:
         copy.start()
 
@@ -492,30 +523,9 @@
     def _():
         lax.fori_loop(0, ROWS // 16, recon_step, 0)
 
-    sends = []
-
-    def send(i, src, dst, where):
-        copy = pltpu.make_async_remote_copy(
-            src_ref=src,
-            dst_ref=dst,
-            send_sem=send_sem.at[i],
-            recv_sem=recv_sem.at[i],
-            device_id=around[where],
-            device_id_type=MESH,
-        )
-        sends.append(copy)
-        return copy
-
-    to_low = send(0, rec.at[:, pl.ds(0, 24), :], xhi, "xlo")
-    to_high = send(1, rec.at[:, pl.ds(ROWS - 24, 24), :], xlo, "xhi")
-
-    @pl.when(has_low & jnp.logical_not(late_low))
-    def _():
-        to_low.start()
-
-    @pl.when(has_high)
-    def _():
-        to_high.start()
+    @pl.when(jnp.logical_not(waits_long))
+    def _():
+        send_x()
 
 
     def turn_to_y(k, carry):

time: 27.1 us -> 26.7 us (0.985); the launches traced: 26.6 us -> 26.6 us
  no operation moved by 1% of the time
where the time goes in v6:
time: 26.7 us; the launch traced here: 26.6 us
  Pallas kernels  24.7 us (93%)
  local copies, waits for them, and re-layouts  1.26 us (5%)
  between operations  0.64 us (2%)
    pallas_call x1, Pallas kernels, body(): pl.pallas_call(functools.partial(kernel, sizes), out_shape=(pltpu.VMEM(pl...  24.7 us
    unnamed x1, local copies, waits for them, and re-layouts  0.75 us

profile of v6, /device:TPU:1, one launch (start us, length us, event | category | flops | bytes accessed | tf_op | source)
XLA Modules:
  0.0 26.6 jit_solution(14426744179025864390)
XLA Ops:
  0.6 24.7 %shard_map.86 = (f32[12,64,128]{2,1,0:T(8,128)S(1)}, f32[8,128]{1,0:T(8,128)S(1)}) custom-call(f32[12,64,128]{2,1,0:T(8,128)} %bitcast.7, s32[64,128]{1,0:T(8,128)} %bitcast.9, s32[2,8,128]{2,1,0:T(8,128)} %pmap_hbm.1, bf16[12,1600]{1,0:T(8,128)(2,1)} %bitcast.8, bf16[800,1600]{1,0:T(8,128)(2,1)} %w2_hbm.1, bf16[400,800]{1,0:T(8,128)(2,1)} %w3_hbm.1, ...), custom_call_target="tpu_custom_call" | custom-call | tf_op jit(solution)/shard_map/pallas_call | solution.py:827
  25.4 0.7 %copy.10 = f32[12,8,8,128]{3,2,1,0:T(8,128)} copy(f32[12,8,8,128]{3,2,1,0:T(8,128)S(1)} %bitcast.6) | data formatting | bytes 786432
  26.1 0.5 %slice_bitcast_fusion = f32[8]{0:T(128)} fusion(f32[8,128]{1,0:T(8,128)S(1)} %get-tuple-element.5), kind=kLoop, calls=%fused_computation | loop fusion | bytes 64 | tf_op jit(solution)/shard_map/squeeze | solution.py:892

commit v7 on v6

--- a/solution.py
+++ b/solution.py
@@ -294,7 +294,7 @@
     def _():
         greet("xhi")
 
-    firsts = half // 8
+    firsts = half // 4 if half >= 8 else 0
     last_at = half // 2
     lasts = half // 4 if firsts else 0
     is_first = rank < firsts

time: 26.7 us -> 28.1 us (1.052)
  Pallas kernels: 24.7 us -> 26.1 us
    pallas_call x1, Pallas kernels: 24.7 us -> 26.1 us  [body(): pl.pallas_call(functools.partial(kernel, sizes), out_shape=(pltpu.VMEM(pl...]
where the time goes in v7:
time: 28.1 us; the launch traced here: 27.9 us
  Pallas kernels  26.1 us (93%)
  local copies, waits for them, and re-layouts  1.26 us (4%)
  between operations  0.64 us (2%)
    pallas_call x1, Pallas kernels, body(): pl.pallas_call(functools.partial(kernel, sizes), out_shape=(pltpu.VMEM(pl...  26.1 us
    unnamed x1, local copies, waits for them, and re-layouts  0.75 us

profile of v7, /device:TPU:1, one launch (start us, length us, event | category | flops | bytes accessed | tf_op | source)
XLA Modules:
  0.0 27.9 jit_solution(5482251768276302168)
XLA Ops:
  0.6 26.1 %shard_map.86 = (f32[12,64,128]{2,1,0:T(8,128)S(1)}, f32[8,128]{1,0:T(8,128)S(1)}) custom-call(f32[12,64,128]{2,1,0:T(8,128)} %bitcast.7, s32[64,128]{1,0:T(8,128)} %bitcast.9, s32[2,8,128]{2,1,0:T(8,128)} %pmap_hbm.1, bf16[12,1600]{1,0:T(8,128)(2,1)} %bitcast.8, bf16[800,1600]{1,0:T(8,128)(2,1)} %w2_hbm.1, bf16[400,800]{1,0:T(8,128)(2,1)} %w3_hbm.1, ...), custom_call_target="tpu_custom_call" | custom-call | tf_op jit(solution)/shard_map/pallas_call | solution.py:827
  26.7 0.7 %copy.10 = f32[12,8,8,128]{3,2,1,0:T(8,128)} copy(f32[12,8,8,128]{3,2,1,0:T(8,128)S(1)} %bitcast.6) | data formatting | bytes 786432
  27.4 0.5 %slice_bitcast_fusion = f32[8]{0:T(128)} fusion(f32[8,128]{1,0:T(8,128)S(1)} %get-tuple-element.5), kind=kLoop, calls=%fused_computation | loop fusion | bytes 64 | tf_op jit(solution)/shard_map/squeeze | solution.py:892
